TPU v7x, 128 devices: a whole 4x4x4 slice. The times are simulated.
128 devices in a mesh: group: 8 (over x, core), member: 16 (over y, z).
Axes of the slice: x: 4, y: 4, z: 4, core: 2. Of those that a mesh axis runs over, the one named last changes fastest.
Arguments:
- amplitudes: bfloat16 [512, 512, 128], P(('group', 'member')), may hold values from -6 to 6
- integrals: bfloat16 [28672, 128, 128], P(('group', 'member')), may hold values from -0.0625 to 0.0625
- task_plan: int32 [28672, 3], P(('group', 'member')), may hold values from 0 to 511, as said below
Outputs:
- residual_tiles: float32 [512, 512, 128], P(('group', 'member'))
Inputs may be any that keep to these rules, and one draw needn't show every extreme that they name: `task_plan`: column 0 is the source tile, column 1 the destination tile, column 2 the executing device as index in the order group, then member. Both tiles of a row lie in the same symmetry block of 64 consecutive tiles, and the executor is a device of the group that holds that block. Every device is the executor of exactly 224 rows. The rows of one device name one executor at most 2 times, and name destination tiles held by one device at most 4 times; both bounds are reached in every draw.
All inputs are finite; a program needn't handle non-finite values.
Results may differ from a plain program's by a relative error of at most 0.0003.
Values may be sent and summed in bfloat16 or wider, within the bound.
A program may use at most 192 MiB of HBM per device.

v0:
```python
import math

import jax
import jax.numpy as jnp
from jax import lax
from jax.sharding import PartitionSpec as P


def place(tiles, labels, target, capacity, devices_all):
    onehot = (target[:, None] == jnp.arange(devices_all, dtype=jnp.int32)[None, :]).astype(
        jnp.int32
    )
    before = jnp.sum(jnp.cumsum(onehot, axis=0) * onehot, axis=1) - 1
    position = target * capacity + before
    sending = (
        jnp.zeros((devices_all * capacity,) + tiles.shape[1:], tiles.dtype).at[position].set(tiles)
    )
    tagged = jnp.zeros((devices_all * capacity, 3), jnp.int32).at[position].set(labels)
    return (sending, tagged)


def deliver(sending, tagged, capacity, groups, members):
    width = sending.shape[-1]
    devices_all = groups * members
    tiles_in, labels_in = (
        lax.all_to_all(
            sending.reshape(devices_all, capacity, width, width),
            ("group", "member"),
            split_axis=0,
            concat_axis=0,
            tiled=True,
        ),
        lax.all_to_all(
            tagged.reshape(devices_all, capacity, 3),
            ("group", "member"),
            split_axis=0,
            concat_axis=0,
            tiled=True,
        ),
    )
    return (
        tiles_in.reshape(devices_all * capacity, width, width),
        labels_in.reshape(devices_all * capacity, 3),
    )


def accumulate(tiles, source, target, block_amps, count_tiles):
    slots = tiles.shape[0]
    width = tiles.shape[-1]
    rows = block_amps.shape[1]
    block = math.gcd(slots, 32)
    turns = slots // block

    def advance(total, pieces):
        piece_tiles, piece_source, piece_target = pieces
        left_rows = jnp.take(block_amps, piece_source, axis=0)
        product = jnp.einsum(
            "brw,bwv->brv", left_rows, piece_tiles, preferred_element_type=jnp.float32
        )
        return (total.at[piece_target].add(product), None)

    start_total = jnp.zeros((count_tiles, rows, width), jnp.float32)
    total, unused = lax.scan(
        advance,
        start_total,
        (
            tiles.reshape(turns, block, width, width),
            source.reshape(turns, block),
            target.reshape(turns, block),
        ),
    )
    return total


def on_device(amplitudes, integrals, task_plan):
    groups = lax.axis_size("group")
    members = lax.axis_size("member")
    devices_all = groups * members
    tile_dev = amplitudes.shape[0]
    tile_grp = tile_dev * members
    tasks = integrals.shape[0]
    peer_cap = (tasks + devices_all - 1) // devices_all
    block_amps = lax.all_gather(amplitudes, "member", axis=0, tiled=True)
    source = task_plan[:, 0] % tile_grp
    valid = jnp.ones((tasks,), jnp.int32)
    target = task_plan[:, 2]
    local_dest = task_plan[:, 1] % tile_grp
    labels = jnp.stack([source, local_dest, valid], axis=1)
    sending, tagged = place(integrals, labels, target, peer_cap, devices_all)
    tiles_in, labels_in = deliver(sending, tagged, peer_cap, groups, members)
    order = jnp.argsort(1 - labels_in[:, 2], stable=True)[:tasks]
    tiles_in = jnp.take(tiles_in, order, axis=0)
    labels_in = jnp.take(labels_in, order, axis=0)
    partial_tiles = accumulate(tiles_in, labels_in[:, 0], labels_in[:, 1], block_amps, tile_grp)
    return lax.psum_scatter(partial_tiles, "member", scatter_dimension=0, tiled=True)


def solution(mesh):
    in_specs = (
        P(("group", "member"), None, None),
        P(("group", "member"), None, None),
        P(("group", "member"), None),
    )
    out_specs = P(("group", "member"), None, None)
    return jax.shard_map(
        on_device, mesh=mesh, in_specs=in_specs, out_specs=out_specs, check_vma=False
    )
```

profile of v0, /device:TPU:1, one launch (start us, length us, event | category | flops | bytes accessed | tf_op | source)
XLA Modules:
  0.0 551.8 jit_solution(9831368002065886652)
XLA Ops:
  11.3 11.5 %all-to-all-start = ((s32[128,2,3]{2,1,0:T(2,128)}), s32[128,2,3]{2,1,0:T(2,128)S(1)}, u32[]{:S(2)}, u32[]{:S(2)}) async-start(s32[128,2,3]{2,1,0:T(2,128)} %bitcast.13), calls=%async_computation | async-start | bytes 262144 | tf_op jit(solution)/shard_map/all_to_all | solution.py:33
  22.8 5.3 broadcast_in_dim.51
  28.1 33.8 %scatter_fusion.1 = bf16[256,128,128]{2,1,0:T(8,128)(2,1)} fusion(bf16[256,128,128]{2,1,0:T(8,128)(2,1)} %broadcast_in_dim.51, s32[224]{0:T(256)S(1)} %bitcast.57, bf16[224,128,128]{2,1,0:T(8,128)(2,1)} %param.6), kind=kCustom, calls=%fused_computation.5 | custom fusion | bytes 22020992 | tf_op jit(solution)/shard_map/scatter | solution.py:16
  61.9 10.2 %all-to-all-start.1 = ((bf16[128,2,128,128]{3,2,1,0:T(8,128)(2,1)}), bf16[128,2,128,128]{3,2,1,0:T(8,128)(2,1)}, u32[]{:S(2)}, u32[]{:S(2)}) async-start(bf16[128,2,128,128]{3,2,1,0:T(8,128)(2,1)} %bitcast.45), calls=%async_computation.1 | async-start | bytes 16777216 | tf_op jit(solution)/shard_map/all_to_all | solution.py:26
  72.5 3.2 sort.17
  76.9 105.0 %all-to-all-done.1 = bf16[128,2,128,128]{3,2,1,0:T(8,128)(2,1)} async-done(((bf16[128,2,128,128]{3,2,1,0:T(8,128)(2,1)}), bf16[128,2,128,128]{3,2,1,0:T(8,128)(2,1)}, u32[]{:S(2)}, u32[]{:S(2)}) %all-to-all-start.1) | async-done | bytes 8388640 | tf_op jit(solution)/shard_map/all_to_all | solution.py:26
  181.9 11.8 %gather_fusion.2 = bf16[224,128,128]{2,1,0:T(8,128)(2,1)} fusion(bf16[256,128,128]{2,1,0:T(8,128)(2,1)} %bitcast.16, s32[1024]{0:T(1024)S(1)} %pad_clamp_fusion.1), kind=kCustom, calls=%fused_computation.2 | custom fusion | bytes 14680960 | tf_op jit(solution)/shard_map/jit(_take)/gather | solution.py:92
  193.7 6.7 %broadcast_select_fusion = bf16[7,32,128,128]{3,2,1,0:T(8,128)(2,1)} fusion(bf16[7,32,128,128]{3,2,1,0:T(8,128)(2,1)} %bitcast.46, pred[7,32]{1,0:T(8,128)(4,1)S(1)} %compare_and_fusion.1), kind=kLoop, calls=%fused_computation.24 | loop fusion | flops 3670016 | bytes 14680288 | tf_op jit(solution)/shard_map/jit(_take)/select_n | solution.py:92
  200.5 7.8 %broadcast_in_dim.45 = f32[64,512,128]{2,1,0:T(8,128)} broadcast(f32[]{:T(128)} %constant.85.clone.1), dimensions={} | broadcast | bytes 16777220 | tf_op jit(solution)/shard_map/broadcast_in_dim | solution.py:62
  208.2 225.0 %while.10 = (s32[]{:T(128)}, f32[64,512,128]{2,1,0:T(8,128)}, s32[7,32]{1,0:T(8,128)S(1)}, s32[7,32]{1,0:T(8,128)S(1)}, bf16[64,512,128]{2,1,0:T(8,128)(2,1)}, /*index=5*/bf16[7,32,128,128]{3,2,1,0:T(8,128)(2,1)}, s32[]{:T(128)}) while((s32[]{:T(128)}, f32[64,512,128]{2,1,0:T(8,128)}, s32[7,32]{1,0:T(8,128)S(1)}, s32[7,32]{1,0:T(8,128)S(1)}, ...), condition=%wide.region_8.9_spmd, body=%wide.region_6.8_spmd.sunk | while | flops 541066624 | bytes 47191200 | solution.py:63
  208.3 6.4 %gather_fusion = bf16[32,512,128]{2,1,0:T(8,128)(2,1)} fusion(bf16[64,512,128]{2,1,0:T(8,128)(2,1)} %get-tuple-element.120, s32[1024]{0:T(1024)S(1)} %pad_clamp_fusion.3), kind=kCustom, calls=%fused_computation.clone.1 | custom fusion | bytes 8388736 | tf_op jit(solution)/shard_map/while/body/eval_jaxpr/jit(_take)/gather | solution.py:56
  214.7 7.0 %fusion.27 = f32[32,512,128]{2,1,0:T(8,128)} fusion(bf16[32,512,128]{2,1,0:T(8,128)(2,1)} %gather_fusion, pred[32]{0:T(512)(128)(4,1)S(1)} %compare_and_fusion.4, bf16[7,32,128,128]{3,2,1,0:T(8,128)(2,1)} %get-tuple-element.121, s32[]{:T(128)S(6)} %copy.16), kind=kOutput, calls=%fused_computation.6.clone.1 | convolution fusion | flops 538968064 | bytes 13631524 | tf_op jit(solution)/shard_map/while/body/eval_jaxpr/brw,bwv->brv/dot_general | solution.py:57
  221.7 18.5 %scatter_fusion = f32[64,512,128]{2,1,0:T(8,128)} fusion(f32[64,512,128]{2,1,0:T(8,128)} %get-tuple-element.110, s32[32]{0:T(128)S(1)} %get-tuple-element.100, f32[32,512,128]{2,1,0:T(8,128)} %fusion.27), kind=kCustom, calls=%fused_computation.3.clone.1 | custom fusion | flops 2097152 | bytes 25165952 | tf_op jit(solution)/shard_map/while/body/eval_jaxpr/scatter-add | solution.py:60
  240.2 6.4 %gather_fusion = bf16[32,512,128]{2,1,0:T(8,128)(2,1)} fusion(bf16[64,512,128]{2,1,0:T(8,128)(2,1)} %get-tuple-element.120, s32[1024]{0:T(1024)S(1)} %pad_clamp_fusion.3), kind=kCustom, calls=%fused_computation.clone.1 | custom fusion | bytes 8388736 | tf_op jit(solution)/shard_map/while/body/eval_jaxpr/jit(_take)/gather | solution.py:56
  246.7 7.0 %fusion.27 = f32[32,512,128]{2,1,0:T(8,128)} fusion(bf16[32,512,128]{2,1,0:T(8,128)(2,1)} %gather_fusion, pred[32]{0:T(512)(128)(4,1)S(1)} %compare_and_fusion.4, bf16[7,32,128,128]{3,2,1,0:T(8,128)(2,1)} %get-tuple-element.121, s32[]{:T(128)S(6)} %copy.16), kind=kOutput, calls=%fused_computation.6.clone.1 | convolution fusion | flops 538968064 | bytes 13631524 | tf_op jit(solution)/shard_map/while/body/eval_jaxpr/brw,bwv->brv/dot_general | solution.py:57
  253.7 18.9 %scatter_fusion = f32[64,512,128]{2,1,0:T(8,128)} fusion(f32[64,512,128]{2,1,0:T(8,128)} %get-tuple-element.110, s32[32]{0:T(128)S(1)} %get-tuple-element.100, f32[32,512,128]{2,1,0:T(8,128)} %fusion.27), kind=kCustom, calls=%fused_computation.3.clone.1 | custom fusion | flops 2097152 | bytes 25165952 | tf_op jit(solution)/shard_map/while/body/eval_jaxpr/scatter-add | solution.py:60
  272.6 6.4 %gather_fusion = bf16[32,512,128]{2,1,0:T(8,128)(2,1)} fusion(bf16[64,512,128]{2,1,0:T(8,128)(2,1)} %get-tuple-element.120, s32[1024]{0:T(1024)S(1)} %pad_clamp_fusion.3), kind=kCustom, calls=%fused_computation.clone.1 | custom fusion | bytes 8388736 | tf_op jit(solution)/shard_map/while/body/eval_jaxpr/jit(_take)/gather | solution.py:56
  279.0 7.0 %fusion.27 = f32[32,512,128]{2,1,0:T(8,128)} fusion(bf16[32,512,128]{2,1,0:T(8,128)(2,1)} %gather_fusion, pred[32]{0:T(512)(128)(4,1)S(1)} %compare_and_fusion.4, bf16[7,32,128,128]{3,2,1,0:T(8,128)(2,1)} %get-tuple-element.121, s32[]{:T(128)S(6)} %copy.16), kind=kOutput, calls=%fused_computation.6.clone.1 | convolution fusion | flops 538968064 | bytes 13631524 | tf_op jit(solution)/shard_map/while/body/eval_jaxpr/brw,bwv->brv/dot_general | solution.py:57
  286.0 18.9 %scatter_fusion = f32[64,512,128]{2,1,0:T(8,128)} fusion(f32[64,512,128]{2,1,0:T(8,128)} %get-tuple-element.110, s32[32]{0:T(128)S(1)} %get-tuple-element.100, f32[32,512,128]{2,1,0:T(8,128)} %fusion.27), kind=kCustom, calls=%fused_computation.3.clone.1 | custom fusion | flops 2097152 | bytes 25165952 | tf_op jit(solution)/shard_map/while/body/eval_jaxpr/scatter-add | solution.py:60
  305.0 6.4 %gather_fusion = bf16[32,512,128]{2,1,0:T(8,128)(2,1)} fusion(bf16[64,512,128]{2,1,0:T(8,128)(2,1)} %get-tuple-element.120, s32[1024]{0:T(1024)S(1)} %pad_clamp_fusion.3), kind=kCustom, calls=%fused_computation.clone.1 | custom fusion | bytes 8388736 | tf_op jit(solution)/shard_map/while/body/eval_jaxpr/jit(_take)/gather | solution.py:56
  311.4 7.0 %fusion.27 = f32[32,512,128]{2,1,0:T(8,128)} fusion(bf16[32,512,128]{2,1,0:T(8,128)(2,1)} %gather_fusion, pred[32]{0:T(512)(128)(4,1)S(1)} %compare_and_fusion.4, bf16[7,32,128,128]{3,2,1,0:T(8,128)(2,1)} %get-tuple-element.121, s32[]{:T(128)S(6)} %copy.16), kind=kOutput, calls=%fused_computation.6.clone.1 | convolution fusion | flops 538968064 | bytes 13631524 | tf_op jit(solution)/shard_map/while/body/eval_jaxpr/brw,bwv->brv/dot_general | solution.py:57
  318.4 18.6 %scatter_fusion = f32[64,512,128]{2,1,0:T(8,128)} fusion(f32[64,512,128]{2,1,0:T(8,128)} %get-tuple-element.110, s32[32]{0:T(128)S(1)} %get-tuple-element.100, f32[32,512,128]{2,1,0:T(8,128)} %fusion.27), kind=kCustom, calls=%fused_computation.3.clone.1 | custom fusion | flops 2097152 | bytes 25165952 | tf_op jit(solution)/shard_map/while/body/eval_jaxpr/scatter-add | solution.py:60
  337.0 6.4 %gather_fusion = bf16[32,512,128]{2,1,0:T(8,128)(2,1)} fusion(bf16[64,512,128]{2,1,0:T(8,128)(2,1)} %get-tuple-element.120, s32[1024]{0:T(1024)S(1)} %pad_clamp_fusion.3), kind=kCustom, calls=%fused_computation.clone.1 | custom fusion | bytes 8388736 | tf_op jit(solution)/shard_map/while/body/eval_jaxpr/jit(_take)/gather | solution.py:56
  343.4 7.0 %fusion.27 = f32[32,512,128]{2,1,0:T(8,128)} fusion(bf16[32,512,128]{2,1,0:T(8,128)(2,1)} %gather_fusion, pred[32]{0:T(512)(128)(4,1)S(1)} %compare_and_fusion.4, bf16[7,32,128,128]{3,2,1,0:T(8,128)(2,1)} %get-tuple-element.121, s32[]{:T(128)S(6)} %copy.16), kind=kOutput, calls=%fused_computation.6.clone.1 | convolution fusion | flops 538968064 | bytes 13631524 | tf_op jit(solution)/shard_map/while/body/eval_jaxpr/brw,bwv->brv/dot_general | solution.py:57
  350.4 18.7 %scatter_fusion = f32[64,512,128]{2,1,0:T(8,128)} fusion(f32[64,512,128]{2,1,0:T(8,128)} %get-tuple-element.110, s32[32]{0:T(128)S(1)} %get-tuple-element.100, f32[32,512,128]{2,1,0:T(8,128)} %fusion.27), kind=kCustom, calls=%fused_computation.3.clone.1 | custom fusion | flops 2097152 | bytes 25165952 | tf_op jit(solution)/shard_map/while/body/eval_jaxpr/scatter-add | solution.py:60
  369.1 6.4 %gather_fusion = bf16[32,512,128]{2,1,0:T(8,128)(2,1)} fusion(bf16[64,512,128]{2,1,0:T(8,128)(2,1)} %get-tuple-element.120, s32[1024]{0:T(1024)S(1)} %pad_clamp_fusion.3), kind=kCustom, calls=%fused_computation.clone.1 | custom fusion | bytes 8388736 | tf_op jit(solution)/shard_map/while/body/eval_jaxpr/jit(_take)/gather | solution.py:56
  375.6 7.0 %fusion.27 = f32[32,512,128]{2,1,0:T(8,128)} fusion(bf16[32,512,128]{2,1,0:T(8,128)(2,1)} %gather_fusion, pred[32]{0:T(512)(128)(4,1)S(1)} %compare_and_fusion.4, bf16[7,32,128,128]{3,2,1,0:T(8,128)(2,1)} %get-tuple-element.121, s32[]{:T(128)S(6)} %copy.16), kind=kOutput, calls=%fused_computation.6.clone.1 | convolution fusion | flops 538968064 | bytes 13631524 | tf_op jit(solution)/shard_map/while/body/eval_jaxpr/brw,bwv->brv/dot_general | solution.py:57
  382.6 18.7 %scatter_fusion = f32[64,512,128]{2,1,0:T(8,128)} fusion(f32[64,512,128]{2,1,0:T(8,128)} %get-tuple-element.110, s32[32]{0:T(128)S(1)} %get-tuple-element.100, f32[32,512,128]{2,1,0:T(8,128)} %fusion.27), kind=kCustom, calls=%fused_computation.3.clone.1 | custom fusion | flops 2097152 | bytes 25165952 | tf_op jit(solution)/shard_map/while/body/eval_jaxpr/scatter-add | solution.py:60
  401.3 6.4 %gather_fusion = bf16[32,512,128]{2,1,0:T(8,128)(2,1)} fusion(bf16[64,512,128]{2,1,0:T(8,128)(2,1)} %get-tuple-element.120, s32[1024]{0:T(1024)S(1)} %pad_clamp_fusion.3), kind=kCustom, calls=%fused_computation.clone.1 | custom fusion | bytes 8388736 | tf_op jit(solution)/shard_map/while/body/eval_jaxpr/jit(_take)/gather | solution.py:56
  407.7 7.0 %fusion.27 = f32[32,512,128]{2,1,0:T(8,128)} fusion(bf16[32,512,128]{2,1,0:T(8,128)(2,1)} %gather_fusion, pred[32]{0:T(512)(128)(4,1)S(1)} %compare_and_fusion.4, bf16[7,32,128,128]{3,2,1,0:T(8,128)(2,1)} %get-tuple-element.121, s32[]{:T(128)S(6)} %copy.16), kind=kOutput, calls=%fused_computation.6.clone.1 | convolution fusion | flops 538968064 | bytes 13631524 | tf_op jit(solution)/shard_map/while/body/eval_jaxpr/brw,bwv->brv/dot_general | solution.py:57
  414.7 18.5 %scatter_fusion = f32[64,512,128]{2,1,0:T(8,128)} fusion(f32[64,512,128]{2,1,0:T(8,128)} %get-tuple-element.110, s32[32]{0:T(128)S(1)} %get-tuple-element.100, f32[32,512,128]{2,1,0:T(8,128)} %fusion.27), kind=kCustom, calls=%fused_computation.3.clone.1 | custom fusion | flops 2097152 | bytes 25165952 | tf_op jit(solution)/shard_map/while/body/eval_jaxpr/scatter-add | solution.py:60
  433.3 111.6 %reduce-scatter.2.cloned.1.call-done = f32[4,512,128]{2,1,0:T(8,128)} async-done(((f32[64,512,128]{2,1,0:T(8,128)}), f32[4,512,128]{2,1,0:T(8,128)}) %reduce-scatter.2.cloned.1.call-update) | async-done | bytes 1048592 | tf_op jit(solution)/shard_map/reduce_scatter | solution.py:95
  (56 shorter events, 6.6 us)
Async XLA Ops:
  6.5 193.9 %all-gather.2.cloned.1.call-start = ((), (), s32[]{:S(2)}) async-start(), calls=%async_computation.3 | async-start | bytes 8912896 | tf_op jit(solution)/shard_map/all_gather | solution.py:83
  11.3 50.6 %all-to-all-start = ((s32[128,2,3]{2,1,0:T(2,128)}), s32[128,2,3]{2,1,0:T(2,128)S(1)}, u32[]{:S(2)}, u32[]{:S(2)}) async-start(s32[128,2,3]{2,1,0:T(2,128)} %bitcast.13), calls=%async_computation | async-start | bytes 262144 | tf_op jit(solution)/shard_map/all_to_all | solution.py:33
  61.9 120.0 %all-to-all-start.1 = ((bf16[128,2,128,128]{3,2,1,0:T(8,128)(2,1)}), bf16[128,2,128,128]{3,2,1,0:T(8,128)(2,1)}, u32[]{:S(2)}, u32[]{:S(2)}) async-start(bf16[128,2,128,128]{3,2,1,0:T(8,128)(2,1)} %bitcast.45), calls=%async_computation.1 | async-start | bytes 16777216 | tf_op jit(solution)/shard_map/all_to_all | solution.py:26
  72.1 472.8 %reduce-scatter.2.cloned.1.call-start = ((), (), s32[]{:S(2)}) async-start(), calls=%async_computation.4 | async-start | bytes 17825792 | tf_op jit(solution)/shard_map/reduce_scatter | solution.py:95
Sparse Core Ops, SparseCore 0:
  9.5 159.3 all-gather.1
  433.4 111.4 reduce-scatter.1
where the time goes:
time: 553 us; the launch traced here: 552 us
  waiting for transfers between devices  217 us (39%)
  other arithmetic  142 us (26%)
  local copies, waits for them, and re-layouts  107 us (19%)
  matrix products  48.9 us (9%)
  starting transfers between devices  21.9 us (4%)
  between operations  13.5 us (2%)
    scatter-add x7, other arithmetic, advance(): return (total.at[piece_target].add(product), None)  131 us
    reduce_scatter x1, waiting for transfers between devices, on_device(): lax.psum_scatter(partial_tiles, 'member', scatter_dimension=0, tiled=True)  112 us
    all_to_all x1, waiting for transfers between devices, deliver(): lax.all_to_all(sending.reshape(devices_all, capacity, width, width), ('gr...  105 us
    dot_general x7, matrix products, advance(): jnp.einsum('brw,bwv->brv', left_rows, piece_tiles, preferred_element_type...  48.9 us
    gather x7, local copies, waits for them, and re-layouts, advance(): left_rows = jnp.take(block_amps, piece_source, axis=0)  45.1 us
    scatter x1, local copies, waits for them, and re-layouts, place(): jnp.zeros((devices_all * capacity,) + tiles.shape[1:], tiles.dtype)  33.8 us
    gather x1, local copies, waits for them, and re-layouts, on_device(): tiles_in = jnp.take(tiles_in, order, axis=0)  11.8 us
    all_to_all x1, starting transfers between devices, deliver(): lax.all_to_all(tagged.reshape(devices_all, capacity, 3), ('group', 'membe...  11.5 us
  transfers between devices with their start and end apart: 4, of which 2 were waited for; matrix products, arithmetic and copies ran while one was open for 12% of the time, Pallas kernels for 0%

commit v1 on v0

v1 whole, which is shorter than its diff:
```python
import jax
import jax.numpy as jnp
from jax import lax
from jax.experimental import pallas as pl
from jax.experimental.pallas import tpu as pltpu
from jax.sharding import PartitionSpec as P

MESH = pl.DeviceIdType.MESH
ANY = pl.BlockSpec(memory_space=pl.ANY)
VMEM = pl.BlockSpec(memory_space=pltpu.VMEM)
SMEM = pl.BlockSpec(memory_space=pltpu.SMEM)

NX, NC, NY, NZ = 4, 2, 4, 4
GROUPS = NX * NC
MEMBERS = NY * NZ
CAP = 32
TILES = 4
BLOCK = MEMBERS * TILES
W = 128
ROWS = 512
CODED = ROWS + 16


def position():
    group = lax.axis_index("group")
    member = lax.axis_index("member")
    return group // NC, lax.rem(group, NC), member // NZ, lax.rem(member, NZ)


def device(x, core, y, z):
    return (x * NC + core, y * NZ + z)


def wrap(value, size):
    return lax.rem(value + size, size)


def send(src, dst, send_sem, recv_sem, target):
    copy = pltpu.make_async_remote_copy(
        src_ref=src, dst_ref=dst, send_sem=send_sem, recv_sem=recv_sem,
        device_id=target, device_id_type=MESH,
    )
    copy.start()
    return copy


def greet(targets):
    barrier = pltpu.get_barrier_semaphore()
    for target in targets:
        pl.semaphore_signal(barrier, inc=1, device_id=target, device_id_type=MESH)
    pl.semaphore_wait(barrier, len(targets))


PEERS = ((1, 0), (3, 0), (2, 0), (1, 1), (3, 1), (2, 1), (0, 1))


def exchange_kernel(
    order, labels, integrals, amps, tiles_out, labels_out, amps_out,
    outgoing, tile_send, tile_recv, label_send, label_recv, amp_send, amp_recv, local_sem,
):
    x, core, y, z = position()
    group = x * NC + core
    member = y * NZ + z

    def across(dx, dc):
        return device(wrap(x + dx, NX), wrap(core + dc, NC), y, z)

    def along(axis, step):
        if axis == 0:
            return device(x, core, wrap(y + step, NY), z)
        return device(x, core, y, wrap(z + step, NZ))

    greet([across(*p) for p in PEERS] + [along(a, s) for a in (0, 1) for s in (1, 2, 3)])

    waits = []
    own = [
        pltpu.make_async_copy(amps, amps_out.at[member], local_sem.at[0]),
        pltpu.make_async_copy(labels.at[group], labels_out.at[group], local_sem.at[1]),
    ]
    for copy in own:
        copy.start()
    first = {}
    count = 0
    for axis in (0, 1):
        half = pl.ds(axis * 2, 2)
        for step in (1, 3, 2):
            first[axis, step] = send(
                amps.at[half], amps_out.at[member, half], amp_send.at[count], amp_recv.at[count], along(axis, step)
            )
            count += 1

    def gather(slot, target):
        @pl.loop(0, CAP)
        def _(t):
            outgoing[slot, t] = integrals[order[target * CAP + t]]

    for k, (dx, dc) in enumerate(PEERS):
        target = wrap(x + dx, NX) * NC + wrap(core + dc, NC)
        gather(k, target)
        waits.append(send(outgoing.at[k], tiles_out.at[group], tile_send.at[k], tile_recv.at[k], across(dx, dc)))
        waits.append(send(labels.at[target], labels_out.at[group], label_send.at[k], label_recv.at[k], across(dx, dc)))
    gather(7, group)
    mine = pltpu.make_async_copy(outgoing.at[7], tiles_out.at[group], local_sem.at[2])
    mine.start()
    own.append(mine)

    for arrived in (0, 1, 3, 2):
        for axis in (0, 1):
            half = pl.ds(axis * 2, 2)
            if arrived == 0:
                where, source = member, amps.at[half]
            else:
                first[axis, arrived].wait_recv()
                back = 4 - arrived
                where = wrap(y + back, NY) * NZ + z if axis == 0 else y * NZ + wrap(z + back, NZ)
                source = amps_out.at[where, half]
            for step in (1, 3, 2):
                waits.append(
                    send(source, amps_out.at[where, half], amp_send.at[count], amp_recv.at[count], along(1 - axis, step))
                )
                count += 1
    for copy in first.values():
        copy.wait_send()
    for copy in own:
        copy.wait()
    for copy in waits:
        copy.wait()


def exchange(order, labels, integrals, amps):
    return pl.pallas_call(
        exchange_kernel,
        out_shape=(
            jax.ShapeDtypeStruct((GROUPS, CAP, W, W), jnp.bfloat16),
            jax.ShapeDtypeStruct((GROUPS, 8, 128), jnp.int32),
            jax.ShapeDtypeStruct((MEMBERS, TILES, ROWS, W), jnp.bfloat16),
        ),
        in_specs=[SMEM, ANY, VMEM, ANY],
        out_specs=(ANY, ANY, ANY),
        scratch_shapes=[
            pltpu.VMEM((8, CAP, W, W), jnp.bfloat16),
            pltpu.SemaphoreType.DMA((7,)),
            pltpu.SemaphoreType.DMA((7,)),
            pltpu.SemaphoreType.DMA((7,)),
            pltpu.SemaphoreType.DMA((7,)),
            pltpu.SemaphoreType.DMA((30,)),
            pltpu.SemaphoreType.DMA((30,)),
            pltpu.SemaphoreType.DMA((3,)),
        ],
        compiler_params=pltpu.CompilerParams(collective_id=0, has_side_effects=True, vmem_limit_bytes=40 << 20),
        name="exchange",
    )(order, labels, integrals, amps)


def encode(value):
    most = jnp.max(jnp.abs(value.reshape(ROWS // 16, 16, W)), axis=0)
    power = jnp.ceil(jnp.log2(jnp.maximum(most, 1e-30)) - 14.999)
    factor = jnp.exp2(-power)
    whole = jnp.round(value.reshape(ROWS // 16, 16, W) * factor[None]).astype(jnp.int32)
    return whole.reshape(ROWS, W).astype(jnp.int16), power.astype(jnp.int32).astype(jnp.int16)


def decode(ref):
    factor = jnp.exp2(ref[pl.ds(ROWS, 16), :].astype(jnp.int32).astype(jnp.float32))
    whole = ref[pl.ds(0, ROWS), :].astype(jnp.int32).astype(jnp.float32)
    return (whole.reshape(ROWS // 16, 16, W) * factor[None]).reshape(ROWS, W)


def write(ref, value):
    whole, power = encode(value)
    ref[pl.ds(0, ROWS), :] = whole
    ref[pl.ds(ROWS, 16), :] = power


def contract_kernel(labels, tiles, amps, out, head, following, total):
    step = pl.program_id(0)

    @pl.when(step == 0)
    def _():
        @pl.loop(0, BLOCK)
        def _(a):
            head[a] = -1

        @pl.loop(0, GROUPS * CAP)
        def _(s):
            label = labels[s // CAP, 0, lax.rem(s, CAP)]

            @pl.when(label > 0)
            def _():
                a = lax.rem(label - 1, BLOCK)
                following[s] = head[a]
                head[a] = s

    half, low, first, second = step // 32, lax.rem(step // 16, 2), lax.rem(step // 4, 4), lax.rem(step, 4)
    owner = jnp.where(half == 0, first * NZ + second, second * NZ + first)
    a = owner * TILES + half * 2 + low

    def source(s):
        return (labels[s // CAP, 0, lax.rem(s, CAP)] - 1) // BLOCK

    total[...] = jnp.zeros_like(total)

    def pair(s):
        t = following[s]

        @pl.when(t < 0)
        def _():
            total[...] += jnp.dot(amps[source(s)], tiles[s], preferred_element_type=jnp.float32)

        @pl.when(t >= 0)
        def _():
            left = jnp.concatenate([amps[source(s)], amps[source(t)]], axis=1)
            right = jnp.concatenate([tiles[s], tiles[t]], axis=0)
            total[...] += jnp.dot(left, right, preferred_element_type=jnp.float32)

        return jnp.where(t < 0, -1, following[jnp.maximum(t, 0)])

    lax.while_loop(lambda s: s >= 0, pair, head[a])
    write(out.at[0], total[...])


def contract(labels, tiles, amps):
    return pl.pallas_call(
        contract_kernel,
        grid=(BLOCK,),
        out_shape=jax.ShapeDtypeStruct((BLOCK, CODED, W), jnp.int16),
        in_specs=[SMEM, VMEM, VMEM],
        out_specs=pl.BlockSpec((1, CODED, W), lambda i: (i, 0, 0)),
        scratch_shapes=[
            pltpu.SMEM((BLOCK,), jnp.int32),
            pltpu.SMEM((GROUPS * CAP,), jnp.int32),
            pltpu.VMEM((ROWS, W), jnp.float32),
        ],
        compiler_params=pltpu.CompilerParams(vmem_limit_bytes=40 << 20),
        name="contract",
    )(labels, tiles.reshape(GROUPS * CAP, W, W), amps.reshape(BLOCK, ROWS, W))


CASES = tuple((h, w) for h in (0, 1) for w in (0, 1))


def scatter_kernel(
    parts, out, held, a_in, b_in, c_out, c_in, summed, coded, d_in, e_in, f_out, f_in,
    held_sem, a_send, a_recv, b_send, b_recv, c_send, c_recv, d_send, d_recv, e_send, e_recv, f_send, f_recv,
):
    x, core, y, z = position()
    at = (y, z)

    def along(axis, step):
        if axis == 0:
            return device(x, core, wrap(y + step, NY), z)
        return device(x, core, y, wrap(z + step, NZ))

    def second_of(h, w, k):
        sense = 1 - 2 * w
        return wrap(at[1 - h] + (2, -sense, sense, 0)[k], 4)

    greet([along(a, s) for a in (0, 1) for s in (1, 3)])
    loads, a_copy, b_copy, c_copy, d_copy, e_copy, f_copy = {}, {}, {}, {}, {}, {}, {}
    for k in range(4):
        for i, (h, w) in enumerate(CASES):
            sense = 1 - 2 * w
            a_copy[i, k] = send(
                parts.at[h, w, wrap(at[h] + 2, 4), second_of(h, w, k)], a_in.at[i, k],
                a_send.at[i, k], a_recv.at[i, k], along(h, sense),
            )
    for i, (h, w) in enumerate(CASES):
        sense = 1 - 2 * w
        for j, p in enumerate((wrap(at[h] + sense, 4), at[h])):
            loads[i, j] = pltpu.make_async_copy(parts.at[h, w, p], held.at[i, j], held_sem.at[i, j])
            loads[i, j].start()
        b_copy[i] = send(
            parts.at[h, w, wrap(at[h] - sense, 4)], b_in.at[i], b_send.at[i], b_recv.at[i], along(h, -sense)
        )
    for i in range(4):
        loads[i, 0].wait()
    for k in range(4):
        for i, (h, w) in enumerate(CASES):
            sense = 1 - 2 * w
            a_copy[i, k].wait()
            write(c_out.at[i, k], decode(a_in.at[i, k]) + decode(held.at[i, 0, second_of(h, w, k)]))
            c_copy[i, k] = send(
                c_out.at[i, k], c_in.at[i, k], c_send.at[i, k], c_recv.at[i, k], along(h, sense)
            )
    for i in range(4):
        loads[i, 1].wait()
        b_copy[i].wait()
    for k in range(4):
        for i, (h, w) in enumerate(CASES):
            sense = 1 - 2 * w
            q = second_of(h, w, k)
            c_copy[i, k].wait()
            value = decode(c_in.at[i, k]) + decode(held.at[i, 1, q]) + decode(b_in.at[i, q])
            if k == 0:
                write(coded.at[i, 0], value)
                d_copy[i] = send(coded.at[i, 0], d_in.at[i], d_send.at[i], d_recv.at[i], along(1 - h, sense))
            elif k == 1:
                write(coded.at[i, 1], value)
                e_copy[i] = send(coded.at[i, 1], e_in.at[i], e_send.at[i], e_recv.at[i], along(1 - h, -sense))
            else:
                summed[i, k - 2] = value
    for i, (h, w) in enumerate(CASES):
        sense = 1 - 2 * w
        d_copy[i].wait()
        write(f_out.at[i], decode(d_in.at[i]) + summed[i, 0])
        f_copy[i] = send(f_out.at[i], f_in.at[i], f_send.at[i], f_recv.at[i], along(1 - h, sense))
    for i, (h, w) in enumerate(CASES):
        e_copy[i].wait()
        f_copy[i].wait()
        out[2 * h + w] = summed[i, 1] + decode(e_in.at[i]) + decode(f_in.at[i])


def scatter(parts):
    tile = (CODED, W)
    dma = pltpu.SemaphoreType.DMA
    return pl.pallas_call(
        scatter_kernel,
        out_shape=jax.ShapeDtypeStruct((TILES, ROWS, W), jnp.float32),
        in_specs=[ANY],
        out_specs=VMEM,
        scratch_shapes=[
            pltpu.VMEM((4, 2, 4) + tile, jnp.int16),
            pltpu.VMEM((4, 4) + tile, jnp.int16),
            pltpu.VMEM((4, 4) + tile, jnp.int16),
            pltpu.VMEM((4, 4) + tile, jnp.int16),
            pltpu.VMEM((4, 4) + tile, jnp.int16),
            pltpu.VMEM((4, 2, ROWS, W), jnp.float32),
            pltpu.VMEM((4, 2) + tile, jnp.int16),
            pltpu.VMEM((4,) + tile, jnp.int16),
            pltpu.VMEM((4,) + tile, jnp.int16),
            pltpu.VMEM((4,) + tile, jnp.int16),
            pltpu.VMEM((4,) + tile, jnp.int16),
            dma((4, 2)),
            dma((4, 4)), dma((4, 4)),
            dma((4,)), dma((4,)),
            dma((4, 4)), dma((4, 4)),
            dma((4,)), dma((4,)),
            dma((4,)), dma((4,)),
            dma((4,)), dma((4,)),
        ],
        compiler_params=pltpu.CompilerParams(collective_id=1, has_side_effects=True, vmem_limit_bytes=40 << 20),
        name="scatter",
    )(parts)


def slots(plan):
    rows = plan.shape[0]
    group = plan[:, 2] // MEMBERS
    row = jnp.arange(rows, dtype=jnp.int32)
    earlier = (group[None, :] == group[:, None]) & (row[None, :] < row[:, None])
    place = group * CAP + jnp.sum(earlier.astype(jnp.int32), axis=1)
    label = 1 + plan[:, 1] % BLOCK + BLOCK * (plan[:, 0] % BLOCK)
    here = jnp.arange(GROUPS * CAP, dtype=jnp.int32)[:, None] == place[None, :]
    order = jnp.sum(jnp.where(here, row[None, :], 0), axis=1)
    labels = jnp.sum(jnp.where(here, label[None, :], 0), axis=1)
    return order, jnp.pad(labels.reshape(GROUPS, 1, CAP), ((0, 0), (0, 7), (0, 128 - CAP)))


def on_device(amplitudes, integrals, task_plan):
    order, labels = slots(task_plan)
    tiles, labels, amps = exchange(order, labels, integrals, amplitudes)
    parts = contract(labels, tiles, amps)
    return scatter(parts.reshape(2, 2, 4, 4, CODED, W))


def solution(mesh):
    in_specs = (
        P(("group", "member"), None, None),
        P(("group", "member"), None, None),
        P(("group", "member"), None),
    )
    out_specs = P(("group", "member"), None, None)
    return jax.shard_map(
        on_device, mesh=mesh, in_specs=in_specs, out_specs=out_specs, check_vma=False
    )
```

time: 553 us -> 216 us (0.39)
  waiting for transfers between devices: 217 us -> 0 us
  Pallas kernels: 0 us -> 202 us
  other arithmetic: 142 us -> 1.15 us
  local copies, waits for them, and re-layouts: 107 us -> 12 us
  matrix products: 48.9 us -> 0 us
  starting transfers between devices: 21.9 us -> 0 us
  between operations: 13.5 us -> 0.06 us
    pallas_call x0 -> x3, Pallas kernels: none -> 202 us  [the longest x1 100 us: exchange(): pl.pallas_call(exchange_kernel, out_shape=(jax.ShapeDtypeStruct((GROUPS,...]
    scatter-add x7 -> x0, other arithmetic: 131 us -> none  [advance(): return (total.at[piece_target].add(product), None)]
    reduce_scatter x1 -> x0, waiting for transfers between devices: 112 us -> none  [on_device(): lax.psum_scatter(partial_tiles, 'member', scatter_dimension=0, tiled=True)]
    all_to_all x2 -> x0, waiting for transfers between devices: 105 us -> none  [the longest x1 105 us: deliver(): lax.all_to_all(sending.reshape(devices_all, capacity, width, width), ('gr...]
    gather x9 -> x0, local copies, waits for them, and re-layouts: 57.6 us -> none  [the longest x7 45.1 us: advance(): left_rows = jnp.take(block_amps, piece_source, axis=0)]
    dot_general x7 -> x0, matrix products: 48.9 us -> none  [advance(): jnp.einsum('brw,bwv->brv', left_rows, piece_tiles, preferred_element_type...]
    scatter x2 -> x0, local copies, waits for them, and re-layouts: 35.5 us -> none  [the longest x1 33.8 us: place(): jnp.zeros((devices_all * capacity,) + tiles.shape[1:], tiles.dtype)]
    all_to_all x2 -> x0, starting transfers between devices: 21.7 us -> none  [the longest x1 11.5 us: deliver(): lax.all_to_all(tagged.reshape(devices_all, capacity, 3), ('group', 'membe...]
  transfers between devices with their start and end apart: 4 -> 0, of which waited for: 2 -> 0; matrix products, arithmetic and copies ran while one was open for 12% -> 0% of each run, Pallas kernels for 0% -> 0%
where the time goes in v1:
time: 216 us; the launch traced here: 215 us
  Pallas kernels  202 us (94%)
  local copies, waits for them, and re-layouts  12 us (6%)
    pallas_call x1, Pallas kernels, exchange(): pl.pallas_call(exchange_kernel, out_shape=(jax.ShapeDtypeStruct((GROUPS,...  100 us
    pallas_call x1, Pallas kernels, scatter(): pl.pallas_call(scatter_kernel, out_shape=jax.ShapeDtypeStruct((TILES, ROW...  51.4 us
    pallas_call x1, Pallas kernels, contract(): pl.pallas_call(contract_kernel, grid=(BLOCK,), out_shape=jax.ShapeDtypeSt...  50.4 us
    unnamed x9, local copies, waits for them, and re-layouts  11.9 us

profile of v1, /device:TPU:1, one launch (start us, length us, event | category | flops | bytes accessed | tf_op | source)
XLA Modules:
  0.0 215.4 jit_solution(13890729816114472914)
XLA Ops:
  0.0 0.8 and_select_fusion
  0.8 0.2 convert_reduce_fusion
  1.0 0.1 select_reduce_fusion
  1.2 0.1 reshape.98
  1.3 0.0 copy-start.2
  1.3 3.1 %copy-done.2 = bf16[224,128,128]{2,1,0:T(8,128)(2,1)S(1)} copy-done((bf16[224,128,128]{2,1,0:T(8,128)(2,1)S(1)}, bf16[224,128,128]{2,1,0:T(8,128)(2,1)}, u32[]{:S(2)}) %copy-start.2) | copy-done | bytes 7340056
  4.4 0.0 copy-start.3
  4.4 1.0 copy-done.3
  5.4 100.5 %exchange.1 = (bf16[8,32,128,128]{3,2,1,0:T(8,128)(2,1)}, s32[8,8,128]{2,1,0:T(8,128)S(1)}, bf16[16,4,512,128]{3,2,1,0:T(8,128)(2,1)}) custom-call(s32[256]{0:T(256)S(1)} %get-tuple-element.12.order, s32[8,8,128]{2,1,0:T(8,128)S(1)} %pad.4.labels, bf16[224,128,128]{2,1,0:T(8,128)(2,1)S(1)} %copy-done.2, bf16[4,512,128]{2,1,0:T(8,128)(2,1)S(1)} %copy-done.3), custom_call_target="tpu_custom_call" | custom-call | tf_op jit(solution)/shard_map/exchange/pallas_call | solution.py:131
  105.9 0.0 copy-start.1
  105.9 3.4 %copy-done.1 = bf16[8,32,128,128]{3,2,1,0:T(8,128)(2,1)S(1)} copy-done((bf16[8,32,128,128]{3,2,1,0:T(8,128)(2,1)S(1)}, bf16[8,32,128,128]{3,2,1,0:T(8,128)(2,1)}, u32[]{:S(2)}) %copy-start.1) | copy-done | bytes 8388632
  109.3 50.4 %contract.1 = s16[64,528,128]{2,1,0:T(8,128)(2,1)} custom-call(s32[8,8,128]{2,1,0:T(8,128)S(1)} %get-tuple-element.8.labels, bf16[256,128,128]{2,1,0:T(8,128)(2,1)S(1)} %bitcast.8, bf16[64,512,128]{2,1,0:T(8,128)(2,1)} %bitcast.9), custom_call_target="tpu_custom_call" | custom-call | tf_op jit(solution)/shard_map/contract/pallas_call | solution.py:223
  159.6 0.0 copy-start
  159.6 3.5 %copy-done = s16[64,528,128]{2,1,0:T(8,128)(2,1)S(1)} copy-done((s16[64,528,128]{2,1,0:T(8,128)(2,1)S(1)}, s16[64,528,128]{2,1,0:T(8,128)(2,1)}, u32[]{:S(2)}) %copy-start) | copy-done | bytes 8650776
  163.1 51.4 %scatter.1 = f32[4,512,128]{2,1,0:T(8,128)S(1)} custom-call(s16[2,2,4,4,528,128]{5,4,3,2,1,0:T(8,128)(2,1)S(1)} %bitcast.7), custom_call_target="tpu_custom_call" | custom-call | tf_op jit(solution)/shard_map/scatter/pallas_call | solution.py:316
  214.5 1.0 copy.5
  (3 shorter events, 0.0 us)
Async XLA Ops:
  1.3 3.1 %copy-start.2 = (bf16[224,128,128]{2,1,0:T(8,128)(2,1)S(1)}, bf16[224,128,128]{2,1,0:T(8,128)(2,1)}, u32[]{:S(2)}) copy-start(bf16[224,128,128]{2,1,0:T(8,128)(2,1)} %integrals.1) | copy-start | bytes 22020100
  4.4 1.0 copy-start.3
  105.9 3.4 %copy-start.1 = (bf16[8,32,128,128]{3,2,1,0:T(8,128)(2,1)S(1)}, bf16[8,32,128,128]{3,2,1,0:T(8,128)(2,1)}, u32[]{:S(2)}) copy-start(bf16[8,32,128,128]{3,2,1,0:T(8,128)(2,1)} %get-tuple-element.9) | copy-start | bytes 25165828
  159.6 3.5 %copy-start = (s16[64,528,128]{2,1,0:T(8,128)(2,1)S(1)}, s16[64,528,128]{2,1,0:T(8,128)(2,1)}, u32[]{:S(2)}) copy-start(s16[64,528,128]{2,1,0:T(8,128)(2,1)} %contract.1) | copy-start | bytes 25952260

commit v2 on v0

v2 whole, which is shorter than its diff:
```python
import jax
import jax.numpy as jnp
from jax import lax
from jax.experimental import pallas as pl
from jax.experimental.pallas import tpu as pltpu
from jax.sharding import PartitionSpec as P

MESH = pl.DeviceIdType.MESH
ANY = pl.BlockSpec(memory_space=pl.ANY)
VMEM = pl.BlockSpec(memory_space=pltpu.VMEM)
SMEM = pl.BlockSpec(memory_space=pltpu.SMEM)

NX, NC, NY, NZ = 4, 2, 4, 4
GROUPS = NX * NC
MEMBERS = NY * NZ
CAP = 32
TILES = 4
BLOCK = MEMBERS * TILES
MEET = 4
W = 128
ROWS = 512
HALF = ROWS // 2
CODED = HALF + 16

PEERS = ((1, 0), (3, 0), (1, 1), (3, 1), (2, 0), (2, 1), (0, 1))
OWN, SIBLING, NEAR, FAR = 7, 6, (0, 1, 2, 3), (4, 5)

CASES = tuple((h, w) for h in (0, 1) for w in (0, 1))


def wrap(value, size):
    return lax.rem(value + size, size)


def encode(value):
    blocks = value.reshape(HALF // 16, 16, W)
    most = jnp.max(jnp.abs(blocks), axis=0)
    power = jnp.ceil(jnp.log2(jnp.maximum(most, 1e-30)) - 14.999)
    whole = jnp.round(blocks * jnp.exp2(-power)[None]).astype(jnp.int32)
    return whole.reshape(HALF, W).astype(jnp.int16), power.astype(jnp.int32).astype(jnp.int16)


def decode(ref):
    factor = jnp.exp2(ref[pl.ds(HALF, 16), :].astype(jnp.int32).astype(jnp.float32))
    whole = ref[pl.ds(0, HALF), :].astype(jnp.int32).astype(jnp.float32)
    return (whole.reshape(HALF // 16, 16, W) * factor[None]).reshape(HALF, W)


def write(ref, value):
    whole, power = encode(value)
    ref[pl.ds(0, HALF), :] = whole
    ref[pl.ds(HALF, 16), :] = power


class Reduce:
    def __init__(self, at, along, pair, parts, bufs, sems, out):
        self.at, self.along, self.pair, self.parts, self.out = at, along, pair, parts, out
        self.a_in, self.b_in, self.c_in, self.summed, self.coded, self.d_in, self.e_in, self.f_in = bufs
        self.sems = sems
        self.copies = {}

    def second(self, i, k):
        h, w = CASES[i]
        sense = 1 - 2 * w
        return wrap(self.at[1 - h] + (2, -sense, sense, 0)[k], 4)

    def send(self, name, src, dst, leg, step, *index):
        send_sem, recv_sem = self.sems[name]
        key = index if len(index) > 1 else index[0]
        copy = pltpu.make_async_remote_copy(
            src_ref=src, dst_ref=dst, send_sem=send_sem.at[key], recv_sem=recv_sem.at[key],
            device_id=self.along(leg, step), device_id_type=MESH,
        )
        copy.start()
        self.copies[(name,) + index] = copy

    def start(self):
        for k in range(4):
            for i, (h, w) in enumerate(CASES):
                sense = 1 - 2 * w
                self.send(
                    "a", self.parts.at[h, w, wrap(self.at[h] + 2, 4), self.second(i, k)], self.a_in.at[i, k], h, sense, i, k
                )
        for i, (h, w) in enumerate(CASES):
            sense = 1 - 2 * w
            self.send("b", self.parts.at[h, w, wrap(self.at[h] - sense, 4)], self.b_in.at[i], h, -sense, i)

    def relay(self):
        for k in range(4):
            for i, (h, w) in enumerate(CASES):
                sense = 1 - 2 * w
                self.copies["a", i, k].wait()
                own = self.parts.at[h, w, wrap(self.at[h] + sense, 4), self.second(i, k)]
                write(self.a_in.at[i, k], decode(self.a_in.at[i, k]) + decode(own))
                self.send("c", self.a_in.at[i, k], self.c_in.at[i, k], h, sense, i, k)

    def turn(self):
        for i in range(4):
            self.copies["b", i].wait()
        for k in range(4):
            for i, (h, w) in enumerate(CASES):
                sense = 1 - 2 * w
                q = self.second(i, k)
                self.copies["c", i, k].wait()
                value = decode(self.c_in.at[i, k]) + decode(self.parts.at[h, w, self.at[h], q]) + decode(self.b_in.at[i, q])
                if k == 0:
                    write(self.coded.at[i, 0], value)
                    self.send("d", self.coded.at[i, 0], self.d_in.at[i], 1 - h, sense, i)
                elif k == 1:
                    write(self.coded.at[i, 1], value)
                    self.send("e", self.coded.at[i, 1], self.e_in.at[i], 1 - h, -sense, i)
                else:
                    self.summed[i, k - 2] = value

    def pass_on(self):
        for i, (h, w) in enumerate(CASES):
            sense = 1 - 2 * w
            self.copies["d", i].wait()
            write(self.d_in.at[i], decode(self.d_in.at[i]) + self.summed[i, 0])
            self.send("f", self.d_in.at[i], self.f_in.at[i], 1 - h, sense, i)

    def finish(self):
        for i, (h, w) in enumerate(CASES):
            self.copies["e", i].wait()
            self.copies["f", i].wait()
            self.summed[i, 1] = self.summed[i, 1] + decode(self.e_in.at[i]) + decode(self.f_in.at[i])
            self.copies["out", i] = pltpu.make_async_copy(
                self.summed.at[i, 1], self.out.at[2 * self.pair + w, pl.ds(h * HALF, HALF)], self.sems["out"].at[i]
            )
            self.copies["out", i].start()

    def close(self):
        for i in range(4):
            self.copies["out", i].wait()


REDUCE_SEMS = (("a", (4, 4)), ("b", (4,)), ("c", (4, 4)), ("d", (4,)), ("e", (4,)), ("f", (4,)))


def reduce_scratch():
    tile = (CODED, W)
    shapes = [
        pltpu.VMEM((2, 2, 4, 4) + tile, jnp.int16),
        pltpu.VMEM((4, 4) + tile, jnp.int16),
        pltpu.VMEM((4, 4) + tile, jnp.int16),
        pltpu.VMEM((4, 4) + tile, jnp.int16),
        pltpu.VMEM((4, 2, HALF, W), jnp.float32),
        pltpu.VMEM((4, 2) + tile, jnp.int16),
        pltpu.VMEM((4,) + tile, jnp.int16),
        pltpu.VMEM((4,) + tile, jnp.int16),
        pltpu.VMEM((4,) + tile, jnp.int16),
    ]
    for _, shape in REDUCE_SEMS:
        shapes += [pltpu.SemaphoreType.DMA(shape)] * 2
    return shapes + [pltpu.SemaphoreType.DMA((4,))]


def ladder_kernel(order, labels, integrals, amps, out, *scratch):
    scratch = list(scratch)

    def take(n):
        taken = scratch[:n]
        del scratch[:n]
        return taken

    stored, outgoing, block_amps, label_in, label_s, total = take(6)
    arrived = take(8)
    tile_send, tile_recv, label_send, label_recv, amp_send, amp_recv, local_sem, smem_sem = take(8)

    group = lax.axis_index("group")
    member = lax.axis_index("member")
    x, core, y, z = group // NC, lax.rem(group, NC), member // NZ, lax.rem(member, NZ)

    def across(k):
        dx, dc = PEERS[k]
        return (wrap(x + dx, NX) * NC + wrap(core + dc, NC), member)

    def along(axis, step):
        if axis == 0:
            return (group, wrap(y + step, NY) * NZ + z)
        return (group, y * NZ + wrap(z + step, NZ))

    sums = []
    for pair in (0, 1):
        parts, *bufs = take(9)
        sems = {name: tuple(take(2)) for name, _ in REDUCE_SEMS}
        (sems["out"],) = take(1)
        sums.append(Reduce((y, z), along, pair, parts, bufs, sems, out))

    load = pltpu.make_async_copy(integrals, stored, local_sem.at[0])
    load.start()
    own_amps = pltpu.make_async_copy(amps, block_amps.at[member], local_sem.at[1])
    own_amps.start()
    own_label = pltpu.make_async_copy(labels.at[group], label_in.at[OWN], local_sem.at[2])
    own_label.start()

    barrier = pltpu.get_barrier_semaphore()
    for k in range(7):
        pl.semaphore_signal(barrier, inc=1, device_id=across(k), device_id_type=MESH)
    for axis in (0, 1):
        for step in (1, 2, 3):
            pl.semaphore_signal(barrier, inc=1, device_id=along(axis, step), device_id_type=MESH)
    pl.semaphore_wait(barrier, 13)

    def send(src, dst, send_sem, recv_sem, target):
        copy = pltpu.make_async_remote_copy(
            src_ref=src, dst_ref=dst, send_sem=send_sem, recv_sem=recv_sem, device_id=target, device_id_type=MESH
        )
        copy.start()
        return copy

    first, others = {}, []
    count = 0
    for axis in (0, 1):
        half = pl.ds(axis * 2, 2)
        for step in (1, 3, 2):
            first[axis, step] = send(
                amps.at[half], block_amps.at[member, half], amp_send.at[count], amp_recv.at[count], along(axis, step)
            )
            count += 1

    load.wait()
    tile_copies, label_copies = [], []
    for k in range(7):
        target = across(k)

        @pl.loop(0, CAP)
        def _(t):
            outgoing[k, t] = stored[order[target[0] * CAP + t]]

        tile_copies.append(send(outgoing.at[k], arrived[k], tile_send.at[k], tile_recv.at[k], target))
        label_copies.append(send(labels.at[target[0]], label_in.at[k], label_send.at[k], label_recv.at[k], target))

    @pl.loop(0, CAP)
    def _(t):
        arrived[OWN][t] = stored[order[group * CAP + t]]

    for came in (0, 1, 3, 2):
        for axis in (0, 1):
            half = pl.ds(axis * 2, 2)
            if came == 0:
                where, source = member, amps.at[half]
            else:
                first[axis, came].wait_recv()
                back = 4 - came
                where = wrap(y + back, NY) * NZ + z if axis == 0 else y * NZ + wrap(z + back, NZ)
                source = block_amps.at[where, half]
            for step in (1, 3, 2):
                others.append(
                    send(source, block_amps.at[where, half], amp_send.at[count], amp_recv.at[count], along(1 - axis, step))
                )
                count += 1

    for k in range(8):
        if k == OWN:
            own_label.wait()
        else:
            label_copies[k].wait()
        move = pltpu.make_async_copy(label_in.at[k], label_s.at[k], smem_sem.at[k])
        move.start()
        move.wait()
    own_amps.wait()
    for copy in first.values():
        copy.wait_send()
    for copy in others:
        copy.wait()

    def contract(pair, sources, opening):
        @pl.loop(0, MEMBERS)
        def _(d):
            left, right = [], []
            for k in sources:
                for j in range(MEET):
                    entry = label_s[k, 0, pair * 64 + d * MEET + j]
                    tile = arrived[k][entry & 31]
                    source = lax.shift_right_logical(entry, 8) & 63
                    column = lax.shift_right_logical(entry, 16)
                    left.append(block_amps[source // TILES, source & 3])
                    none = jnp.zeros_like(tile)
                    right.append(
                        jnp.concatenate([jnp.where(column == 0, tile, none), jnp.where(column == 1, tile, none)], axis=1)
                    )
            product = jnp.dot(
                jnp.concatenate(left, axis=1), jnp.concatenate(right, axis=0), preferred_element_type=jnp.float32
            )
            if opening:
                total[d] = product
            else:
                total[d] += product

    def code(pair):
        @pl.loop(0, MEMBERS)
        def _(d):
            one, two = d // NZ, lax.rem(d, NZ)
            for h, w in CASES:
                p, q = (one, two) if h == 0 else (two, one)
                write(sums[pair].parts.at[h, w, p, q], total[d, pl.ds(h * HALF, HALF), pl.ds(w * W, W)])

    tile_copies[SIBLING].wait()
    contract(0, (OWN, SIBLING), True)
    for k in NEAR:
        tile_copies[k].wait()
    contract(0, NEAR, False)
    for k in FAR:
        tile_copies[k].wait()
    contract(0, FAR, False)
    code(0)
    sums[0].start()
    contract(1, (OWN, SIBLING), True)
    sums[0].relay()
    contract(1, NEAR, False)
    sums[0].turn()
    contract(1, FAR, False)
    code(1)
    sums[1].start()
    sums[0].pass_on()
    sums[0].finish()
    sums[1].relay()
    sums[1].turn()
    sums[1].pass_on()
    sums[1].finish()
    sums[0].close()
    sums[1].close()


def ladder(order, labels, integrals, amps):
    dma = pltpu.SemaphoreType.DMA
    return pl.pallas_call(
        ladder_kernel,
        out_shape=jax.ShapeDtypeStruct((TILES, ROWS, W), jnp.float32),
        in_specs=[SMEM, ANY, ANY, ANY],
        out_specs=ANY,
        scratch_shapes=[
            pltpu.VMEM(integrals.shape, jnp.bfloat16),
            pltpu.VMEM((7, CAP, W, W), jnp.bfloat16),
            pltpu.VMEM((MEMBERS, TILES, ROWS, W), jnp.bfloat16),
            pltpu.VMEM((GROUPS, 8, 128), jnp.int32),
            pltpu.SMEM((GROUPS, 8, 128), jnp.int32),
            pltpu.VMEM((MEMBERS, ROWS, 2 * W), jnp.float32),
        ]
        + [pltpu.VMEM((CAP, W, W), jnp.bfloat16)] * 8
        + [dma((7,)), dma((7,)), dma((7,)), dma((7,)), dma((30,)), dma((30,)), dma((3,)), dma((8,))]
        + reduce_scratch() * 2,
        compiler_params=pltpu.CompilerParams(collective_id=0, has_side_effects=True, vmem_limit_bytes=60 << 20),
        name="ladder",
    )(order, labels, integrals, amps)


def slots(plan):
    rows = plan.shape[0]
    group = plan[:, 2] // MEMBERS
    source = plan[:, 0] % BLOCK
    target = plan[:, 1] % BLOCK
    tile = target % TILES
    row = jnp.arange(rows, dtype=jnp.int32)
    before = row[None, :] < row[:, None]
    here = group[None, :] == group[:, None]
    slot = jnp.sum((here & before).astype(jnp.int32), axis=1)
    meet = group * 128 + (tile // 2) * 64 + (target // TILES) * MEET
    place = meet + jnp.sum(((meet[None, :] == meet[:, None]) & before).astype(jnp.int32), axis=1)
    entry = slot + 256 * source + 65536 * (tile % 2)
    at = jnp.arange(GROUPS * CAP, dtype=jnp.int32)[:, None] == (group * CAP + slot)[None, :]
    order = jnp.sum(jnp.where(at, row[None, :], 0), axis=1)
    at = jnp.arange(GROUPS * 128, dtype=jnp.int32)[:, None] == place[None, :]
    labels = 2 * 65536 + jnp.sum(jnp.where(at, entry[None, :] - 2 * 65536, 0), axis=1)
    return order, jnp.pad(labels.reshape(GROUPS, 1, 128), ((0, 0), (0, 7), (0, 0)))


def on_device(amplitudes, integrals, task_plan):
    order, labels = slots(task_plan)
    return ladder(order, labels, integrals, amplitudes)


def solution(mesh):
    in_specs = (
        P(("group", "member"), None, None),
        P(("group", "member"), None, None),
        P(("group", "member"), None),
    )
    out_specs = P(("group", "member"), None, None)
    return jax.shard_map(
        on_device, mesh=mesh, in_specs=in_specs, out_specs=out_specs, check_vma=False
    )
```

time: 553 us -> 201 us (0.36)
  waiting for transfers between devices: 217 us -> 0 us
  Pallas kernels: 0 us -> 194 us
  other arithmetic: 142 us -> 2 us
  local copies, waits for them, and re-layouts: 107 us -> 2.88 us
  matrix products: 48.9 us -> 0 us
  starting transfers between devices: 21.9 us -> 0 us
  between operations: 13.5 us -> 0.04 us
    pallas_call x0 -> x1, Pallas kernels: none -> 194 us  [ladder(): pl.pallas_call(ladder_kernel, out_shape=jax.ShapeDtypeStruct((TILES, ROWS...]
    scatter-add x7 -> x0, other arithmetic: 131 us -> none  [advance(): return (total.at[piece_target].add(product), None)]
    reduce_scatter x1 -> x0, waiting for transfers between devices: 112 us -> none  [on_device(): lax.psum_scatter(partial_tiles, 'member', scatter_dimension=0, tiled=True)]
    all_to_all x2 -> x0, waiting for transfers between devices: 105 us -> none  [the longest x1 105 us: deliver(): lax.all_to_all(sending.reshape(devices_all, capacity, width, width), ('gr...]
    gather x9 -> x0, local copies, waits for them, and re-layouts: 57.6 us -> none  [the longest x7 45.1 us: advance(): left_rows = jnp.take(block_amps, piece_source, axis=0)]
    dot_general x7 -> x0, matrix products: 48.9 us -> none  [advance(): jnp.einsum('brw,bwv->brv', left_rows, piece_tiles, preferred_element_type...]
    scatter x2 -> x0, local copies, waits for them, and re-layouts: 35.5 us -> none  [the longest x1 33.8 us: place(): jnp.zeros((devices_all * capacity,) + tiles.shape[1:], tiles.dtype)]
    all_to_all x2 -> x0, starting transfers between devices: 21.7 us -> none  [the longest x1 11.5 us: deliver(): lax.all_to_all(tagged.reshape(devices_all, capacity, 3), ('group', 'membe...]
  transfers between devices with their start and end apart: 4 -> 0, of which waited for: 2 -> 0; matrix products, arithmetic and copies ran while one was open for 12% -> 0% of each run, Pallas kernels for 0% -> 0%
where the time goes in v2:
time: 201 us; the launch traced here: 199 us
  Pallas kernels  194 us (97%)
  local copies, waits for them, and re-layouts  2.88 us (1%)
    pallas_call x1, Pallas kernels, ladder(): pl.pallas_call(ladder_kernel, out_shape=jax.ShapeDtypeStruct((TILES, ROWS...  194 us

profile of v2, /device:TPU:1, one launch (start us, length us, event | category | flops | bytes accessed | tf_op | source)
XLA Modules:
  0.0 199.4 jit_solution(13244207160087123153)
XLA Ops:
  0.0 0.8 multiply_add_fusion
  0.9 0.3 convert_reduce_fusion
  1.1 0.7 select_reduce_fusion.1.order
  1.8 0.2 select_reduce_fusion
  2.0 0.6 pad.4.labels
  2.6 194.5 %ladder.1 = f32[4,512,128]{2,1,0:T(8,128)} custom-call(s32[256]{0:T(256)} %select_reduce_fusion.1.order, s32[8,8,128]{2,1,0:T(8,128)} %pad.4.labels, bf16[224,128,128]{2,1,0:T(8,128)(2,1)} %integrals.1, bf16[4,512,128]{2,1,0:T(8,128)(2,1)} %amps.1), custom_call_target="tpu_custom_call" | custom-call | tf_op jit(solution)/shard_map/ladder/pallas_call | solution.py:328
  197.1 2.3 %copy.5 = f32[4,512,128]{2,1,0:T(8,128)} copy(f32[4,512,128]{2,1,0:T(8,128)} %ladder.1) | data formatting | bytes 2097152
  (4 shorter events, 0.1 us)

commit v3 on v2

v3 whole, which is shorter than its diff:
```python
import jax
import jax.numpy as jnp
from jax import lax
from jax.experimental import pallas as pl
from jax.experimental.pallas import tpu as pltpu
from jax.sharding import PartitionSpec as P

MESH = pl.DeviceIdType.MESH
ANY = pl.BlockSpec(memory_space=pl.ANY)
VMEM = pl.BlockSpec(memory_space=pltpu.VMEM)
SMEM = pl.BlockSpec(memory_space=pltpu.SMEM)

NX, NC, NY, NZ = 4, 2, 4, 4
GROUPS = NX * NC
MEMBERS = NY * NZ
CAP = 32
TILES = 4
BLOCK = MEMBERS * TILES
MEET = 4
W = 128
ROWS = 512
HALF = ROWS // 2
CODED = HALF + 16

PEERS = ((1, 0), (3, 0), (1, 1), (3, 1), (0, 1), (2, 0), (2, 1))
NEAR, SIBLING, FAR, OWN = (0, 1, 2, 3), 4, (5, 6), 7
FIRST = NEAR + (SIBLING,)

CASES = tuple((h, w) for h in (0, 1) for w in (0, 1))


def wrap(value, size):
    return lax.rem(value + size, size)


def encode(value):
    blocks = value.reshape(HALF // 16, 16, W)
    most = jnp.max(jnp.abs(blocks), axis=0)
    power = jnp.ceil(jnp.log2(jnp.maximum(most, 1e-30)) - 14.999)
    whole = jnp.round(blocks * jnp.exp2(-power)[None]).astype(jnp.int32)
    return whole.reshape(HALF, W).astype(jnp.int16), power.astype(jnp.int32).astype(jnp.int16)


def decode(ref):
    factor = jnp.exp2(ref[pl.ds(HALF, 16), :].astype(jnp.int32).astype(jnp.float32))
    whole = ref[pl.ds(0, HALF), :].astype(jnp.int32).astype(jnp.float32)
    return (whole.reshape(HALF // 16, 16, W) * factor[None]).reshape(HALF, W)


def write(ref, value):
    whole, power = encode(value)
    ref[pl.ds(0, HALF), :] = whole
    ref[pl.ds(HALF, 16), :] = power


class Reduce:
    def __init__(self, at, along, pair, total, parts, bufs, sems, out):
        self.at, self.along, self.pair, self.total, self.parts, self.out = at, along, pair, total, parts, out
        self.a_in, self.b_in, self.c_in, self.d_in, self.e_in, self.f_in = bufs
        self.sems = sems
        self.copies = {}

    def second(self, i, k):
        h, w = CASES[i]
        sense = 1 - 2 * w
        return wrap(self.at[1 - h] + (2, -sense, sense, 0)[k], 4)

    def send(self, name, src, dst, leg, step, *index):
        send_sem, recv_sem = self.sems[name]
        key = index if len(index) > 1 else index[0]
        copy = pltpu.make_async_remote_copy(
            src_ref=src, dst_ref=dst, send_sem=send_sem.at[key], recv_sem=recv_sem.at[key],
            device_id=self.along(leg, step), device_id_type=MESH,
        )
        copy.start()
        self.copies[(name,) + index] = copy

    def own(self, i, q):
        h, w = CASES[i]
        d = self.at[0] * NZ + q if h == 0 else q * NZ + self.at[1]
        return self.total.at[d, pl.ds(h * HALF, HALF), pl.ds(w * W, W)]

    def code(self):
        @pl.loop(0, 12)
        def _(t):
            r, q = t // 4, lax.rem(t, 4)
            for h, w in CASES:
                p = wrap(self.at[h] + r + 1, 4)
                d = p * NZ + q if h == 0 else q * NZ + p
                write(self.parts.at[h, w, r, q], self.total[d, pl.ds(h * HALF, HALF), pl.ds(w * W, W)])

    def start_far(self):
        for k in range(4):
            for i, (h, w) in enumerate(CASES):
                sense = 1 - 2 * w
                self.send(
                    "a", self.parts.at[h, w, 1, self.second(i, k)], self.a_in.at[i, k], h, sense, i, k
                )

    def start_near(self):
        for i, (h, w) in enumerate(CASES):
            sense = 1 - 2 * w
            self.send("b", self.parts.at[h, w, 1 + sense], self.b_in.at[i], h, -sense, i)

    def relay(self):
        for k in range(4):
            for i, (h, w) in enumerate(CASES):
                sense = 1 - 2 * w
                self.copies["a", i, k].wait()
                own = self.parts.at[h, w, 1 - sense, self.second(i, k)]
                write(self.a_in.at[i, k], decode(self.a_in.at[i, k]) + decode(own))
                self.send("c", self.a_in.at[i, k], self.c_in.at[i, k], h, sense, i, k)

    def turn(self):
        for i in range(4):
            self.copies["b", i].wait()
        for k in range(4):
            for i, (h, w) in enumerate(CASES):
                sense = 1 - 2 * w
                q = self.second(i, k)
                self.copies["c", i, k].wait()
                value = decode(self.c_in.at[i, k]) + self.own(i, q)[...] + decode(self.b_in.at[i, q])
                if k == 0:
                    write(self.a_in.at[i, 0], value)
                    self.send("d", self.a_in.at[i, 0], self.d_in.at[i], 1 - h, sense, i)
                elif k == 1:
                    write(self.a_in.at[i, 1], value)
                    self.send("e", self.a_in.at[i, 1], self.e_in.at[i], 1 - h, -sense, i)
                else:
                    self.own(i, q)[...] = value

    def pass_on(self):
        for i, (h, w) in enumerate(CASES):
            sense = 1 - 2 * w
            self.copies["d", i].wait()
            write(self.d_in.at[i], decode(self.d_in.at[i]) + self.own(i, self.second(i, 2))[...])
            self.send("f", self.d_in.at[i], self.f_in.at[i], 1 - h, sense, i)

    def finish(self):
        for i, (h, w) in enumerate(CASES):
            self.copies["e", i].wait()
            self.copies["f", i].wait()
            own = self.own(i, self.second(i, 3))
            own[...] = own[...] + decode(self.e_in.at[i]) + decode(self.f_in.at[i])
            self.copies["out", i] = pltpu.make_async_copy(
                own, self.out.at[2 * self.pair + w, pl.ds(h * HALF, HALF)], self.sems["out"].at[i]
            )
            self.copies["out", i].start()

    def close(self):
        for i in range(4):
            self.copies["out", i].wait()


REDUCE_SEMS = (("a", (4, 4)), ("b", (4,)), ("c", (4, 4)), ("d", (4,)), ("e", (4,)), ("f", (4,)))


def reduce_scratch():
    tile = (CODED, W)
    shapes = [
        pltpu.VMEM((2, 2, 3, 4) + tile, jnp.int16),
        pltpu.VMEM((4, 4) + tile, jnp.int16),
        pltpu.VMEM((4, 4) + tile, jnp.int16),
        pltpu.VMEM((4, 4) + tile, jnp.int16),
        pltpu.VMEM((4,) + tile, jnp.int16),
        pltpu.VMEM((4,) + tile, jnp.int16),
        pltpu.VMEM((4,) + tile, jnp.int16),
    ]
    for _, shape in REDUCE_SEMS:
        shapes += [pltpu.SemaphoreType.DMA(shape)] * 2
    return shapes + [pltpu.SemaphoreType.DMA((4,))]


def ladder_kernel(order, labels, integrals, amps, out, *scratch):
    scratch = list(scratch)

    def take(n):
        taken = scratch[:n]
        del scratch[:n]
        return taken

    stored, outgoing, block_amps, label_in, label_s, *totals = take(7)
    arrived = take(7) + [stored]
    tile_send, tile_recv, label_send, label_recv, amp_send, amp_recv, local_sem, smem_sem = take(8)

    group = lax.axis_index("group")
    member = lax.axis_index("member")
    x, core, y, z = group // NC, lax.rem(group, NC), member // NZ, lax.rem(member, NZ)

    def across(k):
        dx, dc = PEERS[k]
        return (wrap(x + dx, NX) * NC + wrap(core + dc, NC), member)

    def along(axis, step):
        if axis == 0:
            return (group, wrap(y + step, NY) * NZ + z)
        return (group, y * NZ + wrap(z + step, NZ))

    sums = []
    for pair in (0, 1):
        parts, *bufs = take(7)
        sems = {name: tuple(take(2)) for name, _ in REDUCE_SEMS}
        (sems["out"],) = take(1)
        sums.append(Reduce((y, z), along, pair, totals[pair], parts, bufs, sems, out))

    load = pltpu.make_async_copy(integrals, stored, local_sem.at[0])
    load.start()
    own_amps = pltpu.make_async_copy(amps, block_amps.at[member], local_sem.at[1])
    own_amps.start()
    own_label = pltpu.make_async_copy(labels.at[group], label_in.at[OWN], local_sem.at[2])
    own_label.start()

    barrier = pltpu.get_barrier_semaphore()
    for k in range(7):
        pl.semaphore_signal(barrier, inc=1, device_id=across(k), device_id_type=MESH)
    for axis in (0, 1):
        for step in (1, -1):
            pl.semaphore_signal(barrier, inc=1, device_id=along(axis, step), device_id_type=MESH)
    pl.semaphore_wait(barrier, 11)

    def send(src, dst, send_sem, recv_sem, target):
        copy = pltpu.make_async_remote_copy(
            src_ref=src, dst_ref=dst, send_sem=send_sem, recv_sem=recv_sem, device_id=target, device_id_type=MESH
        )
        copy.start()
        return copy

    sent = []

    def pass_amps(where, tiles, axis, step):
        count = len(sent)
        ref = block_amps.at[where, pl.ds(tiles[0], len(tiles))]
        source = amps.at[pl.ds(tiles[0], len(tiles))] if where is member else ref
        copy = send(source, ref, amp_send.at[count], amp_recv.at[count], along(axis, step))
        sent.append(copy)
        return copy

    def moved(axis, place, step):
        a, b = place
        return (wrap(a + step, 4), b) if axis == 0 else (a, wrap(b + step, 4))

    def index(place):
        return place[0] * NZ + place[1]

    here = (y, z)
    leg_one = {}
    for h in (0, 1):
        for step in (1, -1):
            leg_one[h, step] = pass_amps(member, (2 * h, 2 * h + 1), h, step)

    load.wait()
    tile_copies, label_copies = {}, {}

    def post(k, slot):
        target = across(k)

        @pl.loop(0, CAP)
        def _(t):
            outgoing[slot, t] = stored[order[target[0] * CAP + t]]

        tile_copies[k] = send(outgoing.at[slot], arrived[k], tile_send.at[k], tile_recv.at[k], target)

    for k in FIRST:
        post(k, k)
    for k in range(7):
        target = across(k)
        label_copies[k] = send(labels.at[target[0]], label_in.at[k], label_send.at[k], label_recv.at[k], target)

    leg_two, leg_one_on = {}, {}

    def second_leg(h, b):
        where = member if b == 0 else index(moved(h, here, -b))
        for step in (1, -1):
            leg_two[h, b, step] = pass_amps(where, (2 * h, 2 * h + 1), 1 - h, step)

    for h in (0, 1):
        second_leg(h, 0)
    for h in (0, 1):
        for step in (1, -1):
            leg_one[h, step].wait_recv()
            tile = 2 * h + (step == -1)
            leg_one_on[h, step] = pass_amps(index(moved(h, here, -step)), (tile,), h, step)
            second_leg(h, step)
    leg_two_on = []

    def second_leg_on(h, b):
        for step in (1, -1):
            leg_two[h, b, step].wait_recv()
            tile = 2 * h + (step == -1)
            place = moved(1 - h, moved(h, here, -b), -step)
            leg_two_on.append(pass_amps(index(place), (tile,), 1 - h, step))

    for h in (0, 1):
        second_leg_on(h, 0)
    for h in (0, 1):
        for step in (1, -1):
            leg_one_on[h, step].wait_recv()
        second_leg(h, 2)
    tile_copies[SIBLING].wait_send()
    post(FAR[0], SIBLING)
    for b in (1, -1, 2):
        for h in (0, 1):
            second_leg_on(h, b)
    for k in NEAR:
        tile_copies[k].wait_send()

    own_label.wait()
    for k in range(7):
        label_copies[k].wait()
    move = pltpu.make_async_copy(label_in, label_s, smem_sem)
    move.start()
    move.wait()
    own_amps.wait()
    for copy in leg_two_on:
        copy.wait_recv()
    for copy in sent:
        copy.wait_send()

    def contract(pairs, sources, opening, unroll=1):
        @pl.loop(0, MEMBERS // unroll)
        def _(turn):
            for d in [turn * unroll + u for u in range(unroll)]:
                for pair in pairs:
                    left, right = [], []
                    for k in sources:
                        for j in range(MEET):
                            entry = label_s[k, 0, pair * 64 + d * MEET + j]
                            row = entry & 255
                            tile = arrived[k][jnp.minimum(row, integrals.shape[0] - 1 if k == OWN else CAP - 1)]
                            source = lax.shift_right_logical(entry, 8) & 63
                            column = lax.shift_right_logical(entry, 16)
                            left.append(block_amps[source // TILES, source & 3])
                            none = jnp.zeros_like(tile)
                            right.append(
                                jnp.concatenate([jnp.where(column == 0, tile, none), jnp.where(column == 1, tile, none)], axis=1)
                            )
                    product = jnp.dot(
                        jnp.concatenate(left, axis=1), jnp.concatenate(right, axis=0), preferred_element_type=jnp.float32
                    )
                    if opening:
                        totals[pair][d] = product
                    else:
                        totals[pair][d] += product

    tile_copies[SIBLING].wait_recv()
    post(FAR[1], NEAR[0])
    contract((0, 1), (OWN, SIBLING), True)
    for k in NEAR:
        tile_copies[k].wait_recv()
    contract((0, 1), NEAR, False)
    tile_copies[FAR[0]].wait()
    contract((0, 1), FAR[:1], False, 2)
    tile_copies[FAR[1]].wait()
    contract((0,), FAR[1:], False, 4)
    sums[0].code()
    sums[0].start_far()
    contract((1,), FAR[1:], False, 4)
    sums[1].code()
    sums[0].start_near()
    sums[1].start_far()
    sums[0].relay()
    sums[1].start_near()
    sums[1].relay()
    sums[0].turn()
    sums[1].turn()
    sums[0].pass_on()
    sums[1].pass_on()
    sums[0].finish()
    sums[1].finish()
    sums[0].close()
    sums[1].close()


def ladder(order, labels, integrals, amps):
    dma = pltpu.SemaphoreType.DMA
    return pl.pallas_call(
        ladder_kernel,
        out_shape=jax.ShapeDtypeStruct((TILES, ROWS, W), jnp.float32),
        in_specs=[SMEM, ANY, ANY, ANY],
        out_specs=ANY,
        scratch_shapes=[
            pltpu.VMEM(integrals.shape, jnp.bfloat16),
            pltpu.VMEM((len(FIRST), CAP, W, W), jnp.bfloat16),
            pltpu.VMEM((MEMBERS, TILES, ROWS, W), jnp.bfloat16),
            pltpu.VMEM((GROUPS, 8, 128), jnp.int32),
            pltpu.SMEM((GROUPS, 8, 128), jnp.int32),
            pltpu.VMEM((MEMBERS, ROWS, 2 * W), jnp.float32),
            pltpu.VMEM((MEMBERS, ROWS, 2 * W), jnp.float32),
        ]
        + [pltpu.VMEM((CAP, W, W), jnp.bfloat16)] * 7
        + [dma((7,)), dma((7,)), dma((7,)), dma((7,)), dma((40,)), dma((40,)), dma((3,)), dma]
        + reduce_scratch() * 2,
        compiler_params=pltpu.CompilerParams(collective_id=0, has_side_effects=True, vmem_limit_bytes=60 << 20),
        name="ladder",
    )(order, labels, integrals, amps)


def slots(plan):
    rows = plan.shape[0]
    group = plan[:, 2] // MEMBERS
    source = plan[:, 0] % BLOCK
    target = plan[:, 1] % BLOCK
    tile = target % TILES
    row = jnp.arange(rows, dtype=jnp.int32)
    before = row[None, :] < row[:, None]
    here = group[None, :] == group[:, None]
    slot = jnp.sum((here & before).astype(jnp.int32), axis=1)
    meet = group * 128 + (tile // 2) * 64 + (target // TILES) * MEET
    place = meet + jnp.sum(((meet[None, :] == meet[:, None]) & before).astype(jnp.int32), axis=1)
    stay = group == lax.axis_index("group")
    entry = jnp.where(stay, row, slot) + 256 * source + 65536 * (tile % 2)
    at = jnp.arange(GROUPS * CAP, dtype=jnp.int32)[:, None] == (group * CAP + slot)[None, :]
    order = jnp.sum(jnp.where(at, row[None, :], 0), axis=1)
    at = jnp.arange(GROUPS * 128, dtype=jnp.int32)[:, None] == place[None, :]
    labels = 2 * 65536 + jnp.sum(jnp.where(at, entry[None, :] - 2 * 65536, 0), axis=1)
    return order, jnp.pad(labels.reshape(GROUPS, 1, 128), ((0, 0), (0, 7), (0, 0)))


def on_device(amplitudes, integrals, task_plan):
    order, labels = slots(task_plan)
    return ladder(order, labels, integrals, amplitudes)


def solution(mesh):
    in_specs = (
        P(("group", "member"), None, None),
        P(("group", "member"), None, None),
        P(("group", "member"), None),
    )
    out_specs = P(("group", "member"), None, None)
    return jax.shard_map(
        on_device, mesh=mesh, in_specs=in_specs, out_specs=out_specs, check_vma=False
    )
```

time: 201 us -> 162 us (0.81)
  Pallas kernels: 194 us -> 157 us
    pallas_call x1, Pallas kernels: 194 us -> 157 us  [ladder(): pl.pallas_call(ladder_kernel, out_shape=jax.ShapeDtypeStruct((TILES, ROWS...]
where the time goes in v3:
time: 162 us
  Pallas kernels  157 us (97%)
  local copies, waits for them, and re-layouts  2.88 us (2%)
  other arithmetic  2 us (1%)
    pallas_call x1, Pallas kernels, ladder(): pl.pallas_call(ladder_kernel, out_shape=jax.ShapeDtypeStruct((TILES, ROWS...  157 us

profile of v3, /device:TPU:1, one launch (start us, length us, event | category | flops | bytes accessed | tf_op | source)
XLA Modules:
  0.0 161.7 jit_solution(7352254013624948548)
XLA Ops:
  0.0 0.8 multiply_add_fusion
  0.9 0.3 convert_reduce_fusion
  1.1 0.7 select_reduce_fusion.1.order
  1.9 0.2 select_reduce_fusion
  2.0 0.6 pad.4.labels
  2.7 156.8 %ladder.1 = f32[4,512,128]{2,1,0:T(8,128)} custom-call(s32[256]{0:T(256)} %select_reduce_fusion.1.order, s32[8,8,128]{2,1,0:T(8,128)} %pad.4.labels, bf16[224,128,128]{2,1,0:T(8,128)(2,1)} %integrals.1, bf16[4,512,128]{2,1,0:T(8,128)(2,1)} %amps.1), custom_call_target="tpu_custom_call" | custom-call | tf_op jit(solution)/shard_map/ladder/pallas_call | solution.py:376
  159.4 2.3 %copy.5 = f32[4,512,128]{2,1,0:T(8,128)} copy(f32[4,512,128]{2,1,0:T(8,128)} %ladder.1) | data formatting | bytes 2097152
  (4 shorter events, 0.1 us)

commit v4 on v3

--- a/solution.py
+++ b/solution.py
@@ -1,3 +1,5 @@
+import functools
+
 import jax
 import jax.numpy as jnp
 from jax import lax
@@ -17,6 +19,7 @@
 TILES = 4
 BLOCK = MEMBERS * TILES
 MEET = 4
+EARLY = 26
 W = 128
 ROWS = 512
 HALF = ROWS // 2
@@ -171,8 +174,9 @@
     return shapes + [pltpu.SemaphoreType.DMA((4,))]
 
 
-def ladder_kernel(order, labels, integrals, amps, out, *scratch):
+def ladder_kernel(early, order, labels, integrals, amps, out, excess, *scratch):
     scratch = list(scratch)
+    late = CAP - early
 
     def take(n):
         taken = scratch[:n]
@@ -181,7 +185,10 @@
 
     stored, outgoing, block_amps, label_in, label_s, *totals = take(7)
     arrived = take(7) + [stored]
-    tile_send, tile_recv, label_send, label_recv, amp_send, amp_recv, local_sem, smem_sem = take(8)
+    if late:
+        outgoing_late, *arrived_late = take(8)
+    found, found_send, found_recv = take(3)
+    tile_send, tile_recv, late_send, late_recv, label_send, label_recv, amp_send, amp_recv, local_sem, smem_sem = take(10)
 
     group = lax.axis_index("group")
     member = lax.axis_index("member")
@@ -248,17 +255,39 @@
         for step in (1, -1):
             leg_one[h, step] = pass_amps(member, (2 * h, 2 * h + 1), h, step)
 
+    leg_two, leg_one_on = {}, {}
+
+    def second_leg(h, b):
+        where = member if b == 0 else index(moved(h, here, -b))
+        for step in (1, -1):
+            leg_two[h, b, step] = pass_amps(where, (2 * h, 2 * h + 1), 1 - h, step)
+
+    for h in (0, 1):
+        second_leg(h, 0)
+
     load.wait()
     tile_copies, label_copies = {}, {}
 
     def post(k, slot):
         target = across(k)
 
-        @pl.loop(0, CAP)
+        @pl.loop(0, early)
         def _(t):
             outgoing[slot, t] = stored[order[target[0] * CAP + t]]
 
         tile_copies[k] = send(outgoing.at[slot], arrived[k], tile_send.at[k], tile_recv.at[k], target)
+
+    late_copies = {}
+
+    def post_late(k):
+        if late:
+            late_copies[k] = send(
+                outgoing_late.at[k], arrived_late[k], late_send.at[k], late_recv.at[k], across(k)
+            )
+
+    def await_late(k):
+        if late:
+            late_copies[k].wait()
 
     for k in FIRST:
         post(k, k)
@@ -266,15 +295,6 @@
         target = across(k)
         label_copies[k] = send(labels.at[target[0]], label_in.at[k], label_send.at[k], label_recv.at[k], target)
 
-    leg_two, leg_one_on = {}, {}
-
-    def second_leg(h, b):
-        where = member if b == 0 else index(moved(h, here, -b))
-        for step in (1, -1):
-            leg_two[h, b, step] = pass_amps(where, (2 * h, 2 * h + 1), 1 - h, step)
-
-    for h in (0, 1):
-        second_leg(h, 0)
     for h in (0, 1):
         for step in (1, -1):
             leg_one[h, step].wait_recv()
@@ -301,14 +321,42 @@
     for b in (1, -1, 2):
         for h in (0, 1):
             second_leg_on(h, b)
+    for k in range(7 if late else 0):
+        target = across(k)
+
+        @pl.loop(0, late)
+        def _(t):
+            outgoing_late[k, t] = stored[order[target[0] * CAP + early + t]]
+
+    post_late(SIBLING)
     for k in NEAR:
         tile_copies[k].wait_send()
+    post(FAR[1], NEAR[0])
 
     own_label.wait()
     for k in range(7):
         label_copies[k].wait()
     move = pltpu.make_async_copy(label_in, label_s, smem_sem)
     move.start()
+
+    def tell(place, base, axis, step):
+        return send(found.at[place], found.at[base], found_send.at[base - 1], found_recv.at[base - 1], along(axis, step))
+
+    def tell_neighbours(place, axis):
+        return tell(place, place + 1, axis, 1), tell(place, place + 2, axis, -1)
+
+    def tell_on(place, axis, told):
+        told[0].wait_recv()
+        return tell(place + 1, place + 3, axis, 1)
+
+    def add_up(place, told):
+        told[0].wait_send()
+        told[1].wait()
+        told[2].wait()
+        found[place + 4] = found[place] + found[place + 1] + found[place + 2] + found[place + 3]
+
+    found[0] = jnp.sum(label_in[...], axis=0)
+    told_y = tell_neighbours(0, 0)
     move.wait()
     own_amps.wait()
     for copy in leg_two_on:
@@ -326,7 +374,10 @@
                         for j in range(MEET):
                             entry = label_s[k, 0, pair * 64 + d * MEET + j]
                             row = entry & 255
-                            tile = arrived[k][jnp.minimum(row, integrals.shape[0] - 1 if k == OWN else CAP - 1)]
+                            tile = arrived[k][jnp.minimum(row, integrals.shape[0] - 1 if k == OWN else early - 1)]
+                            if late and pair == 1 and k != OWN:
+                                other = arrived_late[k][jnp.clip(row - early, 0, late - 1)]
+                                tile = jnp.where(row < early, tile, other)
                             source = lax.shift_right_logical(entry, 8) & 63
                             column = lax.shift_right_logical(entry, 16)
                             left.append(block_amps[source // TILES, source & 3])
@@ -343,55 +394,80 @@
                         totals[pair][d] += product
 
     tile_copies[SIBLING].wait_recv()
-    post(FAR[1], NEAR[0])
-    contract((0, 1), (OWN, SIBLING), True)
+    contract((0,), (OWN, SIBLING), True, 2)
+    told_y += (tell_on(0, 0, told_y),)
     for k in NEAR:
         tile_copies[k].wait_recv()
-    contract((0, 1), NEAR, False)
+    contract((0,), NEAR, False, 2)
+    add_up(0, told_y)
+    told_z = tell_neighbours(4, 1)
     tile_copies[FAR[0]].wait()
-    contract((0, 1), FAR[:1], False, 2)
+    contract((0,), FAR[:1], False, 4)
     tile_copies[FAR[1]].wait()
+    for k in NEAR:
+        post_late(k)
     contract((0,), FAR[1:], False, 4)
     sums[0].code()
     sums[0].start_far()
-    contract((1,), FAR[1:], False, 4)
+    await_late(SIBLING)
+    contract((1,), (OWN, SIBLING), True, 2)
+    sums[0].start_near()
+    told_z += (tell_on(4, 1, told_z),)
+    for k in FAR:
+        post_late(k)
+    sums[0].relay()
+    for k in NEAR:
+        await_late(k)
+    contract((1,), NEAR, False, 2)
+    for k in FAR:
+        await_late(k)
+    contract((1,), FAR, False, 2)
     sums[1].code()
-    sums[0].start_near()
     sums[1].start_far()
-    sums[0].relay()
+    sums[0].turn()
     sums[1].start_near()
+    sums[0].pass_on()
     sums[1].relay()
-    sums[0].turn()
+    sums[0].finish()
     sums[1].turn()
-    sums[0].pass_on()
     sums[1].pass_on()
-    sums[0].finish()
+    add_up(4, told_z)
+    report = pltpu.make_async_copy(found.at[8], excess, local_sem.at[0])
+    report.start()
     sums[1].finish()
+    report.wait()
     sums[0].close()
     sums[1].close()
 
 
-def ladder(order, labels, integrals, amps):
+def ladder(early, order, labels, integrals, amps):
     dma = pltpu.SemaphoreType.DMA
+    late = CAP - early
+    tiles = [pltpu.VMEM((7, late, W, W), jnp.bfloat16)] + [pltpu.VMEM((late, W, W), jnp.bfloat16)] * 7
     return pl.pallas_call(
-        ladder_kernel,
-        out_shape=jax.ShapeDtypeStruct((TILES, ROWS, W), jnp.float32),
+        functools.partial(ladder_kernel, early),
+        out_shape=(
+            jax.ShapeDtypeStruct((TILES, ROWS, W), jnp.float32),
+            jax.ShapeDtypeStruct((8, 128), jnp.int32),
+        ),
         in_specs=[SMEM, ANY, ANY, ANY],
-        out_specs=ANY,
+        out_specs=(ANY, ANY),
         scratch_shapes=[
             pltpu.VMEM(integrals.shape, jnp.bfloat16),
-            pltpu.VMEM((len(FIRST), CAP, W, W), jnp.bfloat16),
+            pltpu.VMEM((len(FIRST), early, W, W), jnp.bfloat16),
             pltpu.VMEM((MEMBERS, TILES, ROWS, W), jnp.bfloat16),
             pltpu.VMEM((GROUPS, 8, 128), jnp.int32),
             pltpu.SMEM((GROUPS, 8, 128), jnp.int32),
             pltpu.VMEM((MEMBERS, ROWS, 2 * W), jnp.float32),
             pltpu.VMEM((MEMBERS, ROWS, 2 * W), jnp.float32),
         ]
-        + [pltpu.VMEM((CAP, W, W), jnp.bfloat16)] * 7
-        + [dma((7,)), dma((7,)), dma((7,)), dma((7,)), dma((40,)), dma((40,)), dma((3,)), dma]
+        + [pltpu.VMEM((early, W, W), jnp.bfloat16)] * 7
+        + (tiles if late else [])
+        + [pltpu.VMEM((9, 8, 128), jnp.int32), dma((7,)), dma((7,))]
+        + [dma((7,)), dma((7,)), dma((7,)), dma((7,)), dma((7,)), dma((7,)), dma((40,)), dma((40,)), dma((3,)), dma]
         + reduce_scratch() * 2,
-        compiler_params=pltpu.CompilerParams(collective_id=0, has_side_effects=True, vmem_limit_bytes=60 << 20),
-        name="ladder",
+        compiler_params=pltpu.CompilerParams(collective_id=0 if late else 1, has_side_effects=True, vmem_limit_bytes=60 << 20),
+        name="ladder" if late else "ladder_at_once",
     )(order, labels, integrals, amps)
 
 
@@ -404,8 +480,10 @@
     row = jnp.arange(rows, dtype=jnp.int32)
     before = row[None, :] < row[:, None]
     here = group[None, :] == group[:, None]
-    slot = jnp.sum((here & before).astype(jnp.int32), axis=1)
-    meet = group * 128 + (tile // 2) * 64 + (target // TILES) * MEET
+    pair = tile // 2
+    ahead = (pair[None, :] < pair[:, None]) | ((pair[None, :] == pair[:, None]) & before)
+    slot = jnp.sum((here & ahead).astype(jnp.int32), axis=1)
+    meet = group * 128 + pair * 64 + (target // TILES) * MEET
     place = meet + jnp.sum(((meet[None, :] == meet[:, None]) & before).astype(jnp.int32), axis=1)
     stay = group == lax.axis_index("group")
     entry = jnp.where(stay, row, slot) + 256 * source + 65536 * (tile % 2)
@@ -413,12 +491,19 @@
     order = jnp.sum(jnp.where(at, row[None, :], 0), axis=1)
     at = jnp.arange(GROUPS * 128, dtype=jnp.int32)[:, None] == place[None, :]
     labels = 2 * 65536 + jnp.sum(jnp.where(at, entry[None, :] - 2 * 65536, 0), axis=1)
-    return order, jnp.pad(labels.reshape(GROUPS, 1, 128), ((0, 0), (0, 7), (0, 0)))
+    over = jnp.sum(((pair == 0) & (slot >= EARLY) & ~stay).astype(jnp.int32))
+    labels = jnp.where(jnp.arange(8, dtype=jnp.int32)[None, :, None] == 0, labels.reshape(GROUPS, 1, 128), over)
+    return order, labels
 
 
 def on_device(amplitudes, integrals, task_plan):
     order, labels = slots(task_plan)
-    return ladder(order, labels, integrals, amplitudes)
+    out, excess = ladder(EARLY, order, labels, integrals, amplitudes)
+
+    def all_early():
+        return ladder(CAP, order, labels, integrals, amplitudes)[0]
+
+    return lax.cond(excess[1, 0] > 0, all_early, lambda: out)
 
 
 def solution(mesh):

time: 162 us -> 154 us (0.951)
  Pallas kernels: 157 us -> 148 us
    pallas_call x1, Pallas kernels: 157 us -> 148 us  [ladder(): pl.pallas_call(functools.partial(ladder_kernel, early), out_shape=(jax.Sh...]
where the time goes in v4:
time: 154 us
  Pallas kernels  148 us (96%)
  other arithmetic  2.8 us (2%)
  local copies, waits for them, and re-layouts  2.17 us (1%)
    pallas_call x1, Pallas kernels, ladder(): pl.pallas_call(functools.partial(ladder_kernel, early), out_shape=(jax.Sh...  148 us

profile of v4, /device:TPU:1, one launch (start us, length us, event | category | flops | bytes accessed | tf_op | source)
XLA Modules:
  0.0 153.6 jit_solution(920878883490219892)
XLA Ops:
  0.0 0.0 copy-start
  0.0 0.8 multiply_add_fusion
  0.9 0.3 convert_reduce_fusion
  1.2 0.6 fusion.12
  1.8 0.1 select_reduce_fusion.1.order
  1.9 0.2 select_reduce_fusion
  2.1 0.7 broadcast_select_fusion.labels
  2.8 147.7 %ladder.1 = (f32[4,512,128]{2,1,0:T(8,128)S(1)}, s32[8,128]{1,0:T(8,128)}) custom-call(s32[256]{0:T(256)S(1)} %select_reduce_fusion.1.order, s32[8,8,128]{2,1,0:T(8,128)S(1)} %broadcast_select_fusion.labels, bf16[224,128,128]{2,1,0:T(8,128)(2,1)} %integrals.1, bf16[4,512,128]{2,1,0:T(8,128)(2,1)} %amps.1), custom_call_target="tpu_custom_call" | custom-call | tf_op jit(solution)/shard_map/ladder/pallas_call | solution.py:447
  150.6 1.2 slice.15
  152.4 0.0 copy-done
  152.4 0.2 conditional.1
  152.7 1.0 copy.9
  (4 shorter events, 0.0 us)
Async XLA Ops:
  0.0 152.4 %copy-start = (bf16[4,512,128]{2,1,0:T(8,128)(2,1)S(1)}, bf16[4,512,128]{2,1,0:T(8,128)(2,1)}, u32[]{:S(2)}) copy-start(bf16[4,512,128]{2,1,0:T(8,128)(2,1)} %amps.1) | copy-start | bytes 1572868

commit v5 on v4

--- a/solution.py
+++ b/solution.py
@@ -413,9 +413,9 @@
     contract((1,), (OWN, SIBLING), True, 2)
     sums[0].start_near()
     told_z += (tell_on(4, 1, told_z),)
+    sums[0].relay()
     for k in FAR:
         post_late(k)
-    sums[0].relay()
     for k in NEAR:
         await_late(k)
     contract((1,), NEAR, False, 2)

time: 154 us -> 154 us (level)
  no operation moved by 1% of the time
where the time goes in v5:
time: 154 us
  Pallas kernels  148 us (96%)
  other arithmetic  2.8 us (2%)
  local copies, waits for them, and re-layouts  2.17 us (1%)
    pallas_call x1, Pallas kernels, ladder(): pl.pallas_call(functools.partial(ladder_kernel, early), out_shape=(jax.Sh...  148 us

profile of v5, /device:TPU:1, one launch (start us, length us, event | category | flops | bytes accessed | tf_op | source)
XLA Modules:
  0.0 153.6 jit_solution(16759584786582493338)
XLA Ops:
  0.0 0.0 copy-start
  0.0 0.8 multiply_add_fusion
  0.9 0.3 convert_reduce_fusion
  1.2 0.6 fusion.12
  1.8 0.1 select_reduce_fusion.1.order
  1.9 0.2 select_reduce_fusion
  2.1 0.7 broadcast_select_fusion.labels
  2.8 147.7 %ladder.1 = (f32[4,512,128]{2,1,0:T(8,128)S(1)}, s32[8,128]{1,0:T(8,128)}) custom-call(s32[256]{0:T(256)S(1)} %select_reduce_fusion.1.order, s32[8,8,128]{2,1,0:T(8,128)S(1)} %broadcast_select_fusion.labels, bf16[224,128,128]{2,1,0:T(8,128)(2,1)} %integrals.1, bf16[4,512,128]{2,1,0:T(8,128)(2,1)} %amps.1), custom_call_target="tpu_custom_call" | custom-call | tf_op jit(solution)/shard_map/ladder/pallas_call | solution.py:447
  150.6 1.2 slice.15
  152.4 0.0 copy-done
  152.4 0.2 conditional.1
  152.7 1.0 copy.9
  (4 shorter events, 0.0 us)
Async XLA Ops:
  0.0 152.4 %copy-start = (bf16[4,512,128]{2,1,0:T(8,128)(2,1)S(1)}, bf16[4,512,128]{2,1,0:T(8,128)(2,1)}, u32[]{:S(2)}) copy-start(bf16[4,512,128]{2,1,0:T(8,128)(2,1)} %amps.1) | copy-start | bytes 1572868
